TPU v7x, 256 devices: a whole 4x4x8 slice. The times are simulated.
256 devices in a mesh: site: 16 (over z, core), sector: 16 (over y, x).
Axes of the slice: x: 4, y: 4, z: 8, core: 2. Of those that a mesh axis runs over, the one named last changes fastest.
Arguments:
- site_tensor: float32 [16, 4, 16, 512, 512], P('site', None, 'sector'), may hold values from -0.25 to 0.25
- outcomes: int32 [6, 16, 128], P(None, 'site'), may hold values from 0 to 3
- in_flight: float32 [16, 128, 8192], P('site', None, 'sector'), may hold values from -6 to 6
- prior_logp: float32 [16, 128], P('site'), may hold values from -30 to 0
- entering: float32 [5, 128, 8192], P(None, None, 'sector'), may hold values from -6 to 6
Outputs:
- final_env: float32 [16, 128, 8192], P('site', None, 'sector')
- final_logp: float32 [16, 128], P('site')
All inputs are finite; a program needn't handle non-finite values.
Results may differ from a plain program's by a relative error of at most 0.0003.
Values sent between devices are 32-bit elements; how exact they have to be, the bound alone decides.
A program may use at most 64 MiB of HBM per device.

v0:
```python
import jax
import jax.numpy as jnp
from jax import lax
from jax.sharding import PartitionSpec as P

EPSILON = 1e-06


def passed_along(value, axis, steps):
    count = lax.axis_size(axis)
    initial, last = (max(0, -steps), min(count, count - steps))
    return lax.ppermute(value, axis, [(source, source + steps) for source in range(initial, last)])


def sector_products(state_rows, weights, chosen):
    row_count = state_rows.shape[0]
    outcome_count = weights.shape[0]
    local_count = weights.shape[1]
    width = weights.shape[2]
    hop_count = (outcome_count - 2 + local_count) // local_count
    pieces = [state_rows]
    for hop in range(1, hop_count + 1):
        pieces.append(passed_along(state_rows, "sector", -hop))
    joined = jnp.concatenate(pieces, axis=1)
    stacked = jnp.stack(
        [
            joined[:, count * width : (count + local_count) * width]
            for count in range(outcome_count)
        ],
        axis=1,
    )
    stacked = stacked.reshape(row_count, outcome_count, local_count, width)
    amplitude = jnp.einsum("rnsi,nsij->rnsj", stacked, weights, precision=lax.Precision.HIGHEST)
    selector = (chosen[:, None] == jnp.arange(outcome_count, dtype=jnp.int32)[None, :]).astype(
        jnp.float32
    )
    powers = jnp.sum(amplitude * amplitude, axis=(2, 3))
    picked_part = jnp.sum(powers * selector, axis=1)
    total_part = jnp.sum(powers, axis=1)
    selected = jnp.sum(amplitude * selector[:, :, None, None], axis=1)
    return (selected.reshape(row_count, -1), picked_part, total_part)


def step_now(state_rows, log_weight, chosen, weights, bond_size):
    selected, picked_part, total_part = sector_products(state_rows, weights, chosen)
    picked_sum, total_sum = lax.psum((picked_part, total_part), "sector")
    picked_mean = picked_sum / bond_size + EPSILON
    total_mean = total_sum / bond_size + EPSILON
    normalized = selected * lax.rsqrt(picked_mean)[:, None]
    return (normalized, log_weight + jnp.log(picked_mean) - jnp.log(total_mean))


def per_device(site_tensor, outcomes, in_flight, prior_logp, entering):
    weights = site_tensor[0]
    at_start = lax.axis_index("site") == 0
    total_rows = in_flight.shape[1]
    batch_count = 1
    batch_rows = total_rows // batch_count
    bond_size = in_flight.shape[2] * lax.axis_size("sector")
    tick_count = outcomes.shape[0]
    starts = [0]
    states = [in_flight[0, row_start : row_start + batch_rows] for row_start in starts]
    weights_sum = [prior_logp[0, row_start : row_start + batch_rows] for row_start in starts]
    for tick_index in range(tick_count):
        row_start = starts[0]
        state_rows = states[0]
        log_weight = weights_sum[0]
        if tick_index > 0:
            state_rows, log_weight = passed_along((state_rows, log_weight), "site", 1)
            state_rows = jnp.where(
                at_start, entering[tick_index - 1, row_start : row_start + batch_rows], state_rows
            )
            log_weight = jnp.where(at_start, jnp.zeros_like(log_weight), log_weight)
        chosen = outcomes[tick_index, 0, row_start : row_start + batch_rows]
        state_rows, log_weight = step_now(state_rows, log_weight, chosen, weights, bond_size)
        states[0] = state_rows
        weights_sum[0] = log_weight
    final_env = states[0][None]
    final_logp = weights_sum[0][None]
    return (final_env, final_logp)


def solution(mesh):
    return jax.shard_map(
        per_device,
        mesh=mesh,
        in_specs=(
            P("site", None, "sector", None, None),
            P(None, "site", None),
            P("site", None, "sector"),
            P("site", None),
            P(None, None, "sector"),
        ),
        out_specs=(P("site", None, "sector"), P("site", None)),
        check_vma=False,
    )
```

profile of v0, /device:TPU:2, one launch (start us, length us, event | category | flops | bytes accessed | tf_op | source)
XLA Modules:
  0.0 427.4 jit_solution(483862568917737663)
XLA Ops:
  0.6 4.3 %collective-permute-start = (f32[128,512]{1,0:T(8,128)}, f32[128,512]{1,0:T(8,128)S(1)}, u32[]{:S(2)}, u32[]{:S(2)}) collective-permute-start(f32[128,512]{1,0:T(8,128)} %bitcast.133), channel_id=1, source_target_pairs={{1,0},{2,1},{3,2},{4,3},{5,4},{6,5},{7,6},{8,7},{9,8},{10,9},{11,1... | collective-permute-start | bytes 786440 | tf_op jit(solution)/shard_map/ppermute | solution.py:12
  5.0 1.3 collective-permute-start.1
  6.3 1.3 collective-permute-start.2
  8.3 2.8 collective-permute-done
  11.1 6.3 %collective-permute-done.1 = f32[128,512]{1,0:T(8,128)S(1)} collective-permute-done((f32[128,512]{1,0:T(8,128)}, f32[128,512]{1,0:T(8,128)S(1)}, u32[]{:S(2)}, u32[]{:S(2)}) %collective-permute-start.1) | collective-permute-done | bytes 262176 | tf_op jit(solution)/shard_map/ppermute | solution.py:12
  17.5 3.7 collective-permute-done.2
  21.2 4.9 %multiply_reduce_fusion.16 = (f32[128]{0:T(128)S(1)}, f32[128,4]{0,1:T(4,128)S(1)}, f32[128,512]{1,0:T(8,128)S(1)}) fusion(f32[128,4]{0,1:T(4,128)S(1)} %fusion.77, f32[1,4,1,512,512]{4,3,2,1,0:T(8,128)} %param.5, f32[128,1,512]{2,0,1:T(8,128)S(1)} %bitcast.140, f32[128,1,512]{2,0,1:T(8,128)S(1)} %bitcast.138, f32[128,1,512]{2,0,1:T(8,128)S(1)} %bitcast.137, ...), kind=kOutput, calls=%fused_computation.76 | convolution fusion | flops 1612643712 | bytes 5509632 | tf_op jit(solution)/shard_map/rnsi,nsij->rnsj/dot_general | solution.py:33
  26.1 37.8 %psum.84 = f32[128]{0:T(128)S(1)} all-reduce(f32[128]{0:T(128)S(1)} %select_reduce_fusion.5), channel_id=1, replica_groups=mesh['site'=16,'sector'=16] {'sector'}, use_global_device_ids=true, to_apply=%region_3.0 | all-reduce | flops 128 | bytes 1024 | tf_op jit(solution)/shard_map/psum | solution.py:46
  64.1 1.3 collective-permute-start.3
  65.4 1.1 collective-permute-done.3
  66.5 3.6 collective-permute-start.4
  70.2 1.3 collective-permute-start.5
  71.5 1.3 collective-permute-start.6
  72.8 2.0 collective-permute-done.4
  74.8 5.2 %collective-permute-done.5 = f32[128,512]{1,0:T(8,128)S(1)} collective-permute-done((f32[128,512]{1,0:T(8,128)S(1)}, f32[128,512]{1,0:T(8,128)S(1)}, u32[]{:S(2)}, u32[]{:S(2)}) %collective-permute-start.5) | collective-permute-done | bytes 262176 | tf_op jit(solution)/shard_map/ppermute | solution.py:12
  80.0 4.5 %collective-permute-done.6 = f32[128,512]{1,0:T(8,128)S(1)} collective-permute-done((f32[128,512]{1,0:T(8,128)S(1)}, f32[128,512]{1,0:T(8,128)S(1)}, u32[]{:S(2)}, u32[]{:S(2)}) %collective-permute-start.6) | collective-permute-done | bytes 262176 | tf_op jit(solution)/shard_map/ppermute | solution.py:12
  84.6 4.8 %multiply_reduce_fusion.14 = (f32[128]{0:T(128)S(1)}, f32[128,4]{0,1:T(4,128)S(1)}, f32[128,512]{1,0:T(8,128)S(1)}) fusion(f32[128,4]{0,1:T(4,128)S(1)} %fusion.76, f32[1,4,1,512,512]{4,3,2,1,0:T(8,128)} %param.5, f32[128,1,512]{2,0,1:T(8,128)S(1)} %bitcast.151, f32[128,1,512]{2,0,1:T(8,128)S(1)} %bitcast.146, f32[128,1,512]{2,0,1:T(8,128)S(1)} %bitcast.141, ...), kind=kOutput, calls=%fused_computation.74 | convolution fusion | flops 1612643712 | bytes 5509632 | tf_op jit(solution)/shard_map/rnsi,nsij->rnsj/dot_general | solution.py:33
  89.5 38.7 %psum.85 = f32[128]{0:T(128)S(1)} all-reduce(f32[128]{0:T(128)S(1)} %select_reduce_fusion.4), channel_id=1, replica_groups=mesh['site'=16,'sector'=16] {'sector'}, use_global_device_ids=true, to_apply=%region_7.8 | all-reduce | flops 128 | bytes 1024 | tf_op jit(solution)/shard_map/psum | solution.py:46
  128.3 1.3 collective-permute-start.7
  129.6 1.1 collective-permute-done.7
  130.7 1.9 collective-permute-start.8
  132.7 1.3 collective-permute-start.9
  134.0 1.3 collective-permute-start.10
  135.3 3.7 collective-permute-done.8
  139.0 3.8 collective-permute-done.9
  142.8 4.0 collective-permute-done.10
  146.7 4.8 %multiply_reduce_fusion.12 = (f32[128]{0:T(128)S(1)}, f32[128,4]{0,1:T(4,128)S(1)}, f32[128,512]{1,0:T(8,128)S(1)}) fusion(f32[128,4]{0,1:T(4,128)S(1)} %fusion.75, f32[1,4,1,512,512]{4,3,2,1,0:T(8,128)} %param.5, f32[128,1,512]{2,0,1:T(8,128)S(1)} %bitcast.152, f32[128,1,512]{2,0,1:T(8,128)S(1)} %bitcast.147, f32[128,1,512]{2,0,1:T(8,128)S(1)} %bitcast.142, ...), kind=kOutput, calls=%fused_computation.72 | convolution fusion | flops 1612643712 | bytes 5509632 | tf_op jit(solution)/shard_map/rnsi,nsij->rnsj/dot_general | solution.py:33
  151.6 34.5 %psum.86 = f32[128]{0:T(128)S(1)} all-reduce(f32[128]{0:T(128)S(1)} %select_reduce_fusion.3), channel_id=1, replica_groups=mesh['site'=16,'sector'=16] {'sector'}, use_global_device_ids=true, to_apply=%region_11.12 | all-reduce | flops 128 | bytes 1024 | tf_op jit(solution)/shard_map/psum | solution.py:46
  186.2 4.0 collective-permute-start.11
  190.2 1.1 collective-permute-done.11
  191.4 3.0 collective-permute-start.12
  194.4 1.3 collective-permute-start.13
  195.7 1.5 collective-permute-start.14
  197.2 2.5 collective-permute-done.12
  199.7 4.5 %collective-permute-done.13 = f32[128,512]{1,0:T(8,128)S(1)} collective-permute-done((f32[128,512]{1,0:T(8,128)S(1)}, f32[128,512]{1,0:T(8,128)S(1)}, u32[]{:S(2)}, u32[]{:S(2)}) %collective-permute-start.13) | collective-permute-done | bytes 262176 | tf_op jit(solution)/shard_map/ppermute | solution.py:12
  204.2 3.3 collective-permute-done.14
  207.4 4.8 %multiply_reduce_fusion.10 = (f32[128]{0:T(128)S(1)}, f32[128,4]{0,1:T(4,128)S(1)}, f32[128,512]{1,0:T(8,128)S(1)}) fusion(f32[128,4]{0,1:T(4,128)S(1)} %fusion.74, f32[1,4,1,512,512]{4,3,2,1,0:T(8,128)} %param.5, f32[128,1,512]{2,0,1:T(8,128)S(1)} %bitcast.153, f32[128,1,512]{2,0,1:T(8,128)S(1)} %bitcast.148, f32[128,1,512]{2,0,1:T(8,128)S(1)} %bitcast.143, ...), kind=kOutput, calls=%fused_computation.70 | convolution fusion | flops 1612643712 | bytes 5509632 | tf_op jit(solution)/shard_map/rnsi,nsij->rnsj/dot_general | solution.py:33
  212.3 35.4 %psum.87 = f32[128]{0:T(128)S(1)} all-reduce(f32[128]{0:T(128)S(1)} %select_reduce_fusion.2), channel_id=1, replica_groups=mesh['site'=16,'sector'=16] {'sector'}, use_global_device_ids=true, to_apply=%region_15.16 | all-reduce | flops 128 | bytes 1024 | tf_op jit(solution)/shard_map/psum | solution.py:46
  247.8 10.1 %collective-permute-start.15 = (f32[128,512]{1,0:T(8,128)S(1)}, f32[128,512]{1,0:T(8,128)S(1)}, u32[]{:S(2)}, u32[]{:S(2)}) collective-permute-start(f32[128,512]{1,0:T(8,128)S(1)} %broadcast_multiply_fusion.1), channel_id=1, source_target_pairs={{0,16},{16,32},{32,48},{48,64},{64,80},{80,96},{96,112},{112,128},... | collective-permute-start | bytes 786440 | tf_op jit(solution)/shard_map/ppermute | solution.py:12
  257.9 1.1 collective-permute-done.15
  259.1 3.4 collective-permute-start.16
  262.5 1.3 collective-permute-start.17
  263.8 1.3 collective-permute-start.18
  265.1 2.2 collective-permute-done.16
  267.4 4.9 %collective-permute-done.17 = f32[128,512]{1,0:T(8,128)S(1)} collective-permute-done((f32[128,512]{1,0:T(8,128)S(1)}, f32[128,512]{1,0:T(8,128)S(1)}, u32[]{:S(2)}, u32[]{:S(2)}) %collective-permute-start.17) | collective-permute-done | bytes 262176 | tf_op jit(solution)/shard_map/ppermute | solution.py:12
  272.3 2.8 collective-permute-done.18
  275.1 4.8 %multiply_reduce_fusion.8 = (f32[128]{0:T(128)S(1)}, f32[128,4]{0,1:T(4,128)S(1)}, f32[128,512]{1,0:T(8,128)S(1)}) fusion(f32[128,4]{0,1:T(4,128)S(1)} %fusion.73, f32[1,4,1,512,512]{4,3,2,1,0:T(8,128)} %param.5, f32[128,1,512]{2,0,1:T(8,128)S(1)} %bitcast.154, f32[128,1,512]{2,0,1:T(8,128)S(1)} %bitcast.149, f32[128,1,512]{2,0,1:T(8,128)S(1)} %bitcast.144, ...), kind=kOutput, calls=%fused_computation.68 | convolution fusion | flops 1612643712 | bytes 5509632 | tf_op jit(solution)/shard_map/rnsi,nsij->rnsj/dot_general | solution.py:33
  280.0 35.8 %psum.88 = f32[128]{0:T(128)S(1)} all-reduce(f32[128]{0:T(128)S(1)} %select_reduce_fusion.1), channel_id=1, replica_groups=mesh['site'=16,'sector'=16] {'sector'}, use_global_device_ids=true, to_apply=%region_19.20 | all-reduce | flops 128 | bytes 1024 | tf_op jit(solution)/shard_map/psum | solution.py:46
  315.9 11.6 %collective-permute-start.19 = (f32[128,512]{1,0:T(8,128)S(1)}, f32[128,512]{1,0:T(8,128)S(1)}, u32[]{:S(2)}, u32[]{:S(2)}) collective-permute-start(f32[128,512]{1,0:T(8,128)S(1)} %broadcast_multiply_fusion), channel_id=1, source_target_pairs={{0,16},{16,32},{32,48},{48,64},{64,80},{80,96},{96,112},{112,128},... | collective-permute-start | bytes 786440 | tf_op jit(solution)/shard_map/ppermute | solution.py:12
  327.5 1.1 collective-permute-done.19
  328.7 3.0 collective-permute-start.20
  331.7 1.3 collective-permute-start.21
  333.0 1.3 collective-permute-start.22
  334.3 2.6 collective-permute-done.20
  337.0 4.5 %collective-permute-done.21 = f32[128,512]{1,0:T(8,128)S(1)} collective-permute-done((f32[128,512]{1,0:T(8,128)S(1)}, f32[128,512]{1,0:T(8,128)S(1)}, u32[]{:S(2)}, u32[]{:S(2)}) %collective-permute-start.21) | collective-permute-done | bytes 262176 | tf_op jit(solution)/shard_map/ppermute | solution.py:12
  341.5 3.2 collective-permute-done.22
  344.7 4.8 %multiply_reduce_fusion.6 = (f32[128]{0:T(128)S(1)}, f32[128,4]{0,1:T(4,128)S(1)}, f32[128,512]{1,0:T(8,128)S(1)}) fusion(f32[128,4]{0,1:T(4,128)S(1)} %fusion.72, f32[1,4,1,512,512]{4,3,2,1,0:T(8,128)} %param.5, f32[128,1,512]{2,0,1:T(8,128)S(1)} %bitcast.150, f32[128,1,512]{2,0,1:T(8,128)S(1)} %bitcast.145, f32[128,1,512]{2,0,1:T(8,128)S(1)} %bitcast.139, ...), kind=kOutput, calls=%fused_computation.66 | convolution fusion | flops 1612643712 | bytes 5509632 | tf_op jit(solution)/shard_map/rnsi,nsij->rnsj/dot_general | solution.py:33
  349.6 35.4 %all-reduce = (f32[128]{0:T(128)S(1)}, f32[128]{0:T(128)S(1)}, f32[128]{0:T(128)S(1)}, f32[128]{0:T(128)S(1)}, f32[128]{0:T(128)S(1)}, /*index=5*/f32[128]{0:T(128)S(1)}, f32[128]{0:T(128)S(1)}) all-reduce(f32[128]{0:T(128)S(1)} %select_reduce_fusion, ...), channel_id=1, replica_groups=mesh['site'=16,'sector'=16] {'sector'}, use_global_device_ids=true, to_apply=%region_23.24 | all-reduce | flops 896 | bytes 7168 | tf_op jit(solution)/shard_map/psum | solution.py:46
  385.0 10.1 %collective-permute-start.23 = (f32[128]{0:T(128)S(1)}, f32[128]{0:T(128)S(1)}, u32[]{:S(2)}, u32[]{:S(2)}) collective-permute-start(f32[128]{0:T(128)S(1)} %fusion.88), channel_id=1, source_target_pairs={{0,16},{16,32},{32,48},{48,64},{64,80},{80,96},{96,112},{112,128},... | collective-permute-start | bytes 1544 | tf_op jit(solution)/shard_map/ppermute | solution.py:12
  395.9 14.8 %collective-permute-start.24 = (f32[128]{0:T(128)S(1)}, f32[128]{0:T(128)S(1)}, u32[]{:S(2)}, u32[]{:S(2)}) collective-permute-start(f32[128]{0:T(128)S(1)} %fusion.79), channel_id=1, source_target_pairs={{0,16},{16,32},{32,48},{48,64},{64,80},{80,96},{96,112},{112,128},... | collective-permute-start | bytes 1544 | tf_op jit(solution)/shard_map/ppermute | solution.py:12
  411.5 4.1 collective-permute-start.25
  415.6 0.8 collective-permute-done.25
  416.4 4.1 collective-permute-start.26
  421.3 4.1 collective-permute-start.27
  (43 shorter events, 6.1 us)
Async XLA Ops:
  0.6 65.9 %copy-start = (f32[5,128,512]{2,1,0:T(8,128)S(1)}, f32[5,128,512]{2,1,0:T(8,128)}, u32[]{:S(2)}) copy-start(f32[5,128,512]{2,1,0:T(8,128)} %param.9) | copy-start | bytes 3932164
  0.6 10.5 %collective-permute-start = (f32[128,512]{1,0:T(8,128)}, f32[128,512]{1,0:T(8,128)S(1)}, u32[]{:S(2)}, u32[]{:S(2)}) collective-permute-start(f32[128,512]{1,0:T(8,128)} %bitcast.133), channel_id=1, source_target_pairs={{1,0},{2,1},{3,2},{4,3},{5,4},{6,5},{7,6},{8,7},{9,8},{10,9},{11,1... | collective-permute-start | bytes 786440 | tf_op jit(solution)/shard_map/ppermute | solution.py:12
  5.0 12.5 %collective-permute-start.1 = (f32[128,512]{1,0:T(8,128)}, f32[128,512]{1,0:T(8,128)S(1)}, u32[]{:S(2)}, u32[]{:S(2)}) collective-permute-start(f32[128,512]{1,0:T(8,128)} %bitcast.134), channel_id=1, source_target_pairs={{2,0},{3,1},{4,2},{5,3},{6,4},{7,5},{8,6},{9,7},{10,8},{11,9},{12,... | collective-permute-start | bytes 786440 | tf_op jit(solution)/shard_map/ppermute | solution.py:12
  6.3 14.9 %collective-permute-start.2 = (f32[128,512]{1,0:T(8,128)}, f32[128,512]{1,0:T(8,128)S(1)}, u32[]{:S(2)}, u32[]{:S(2)}) collective-permute-start(f32[128,512]{1,0:T(8,128)} %bitcast.135), channel_id=1, source_target_pairs={{3,0},{4,1},{5,2},{6,3},{7,4},{8,5},{9,6},{10,7},{11,8},{12,9},{13... | collective-permute-start | bytes 786440 | tf_op jit(solution)/shard_map/ppermute | solution.py:12
  64.1 2.4 collective-permute-start.3
  66.5 8.3 %collective-permute-start.4 = (f32[128,512]{1,0:T(8,128)S(1)}, f32[128,512]{1,0:T(8,128)S(1)}, u32[]{:S(2)}, u32[]{:S(2)}) collective-permute-start(f32[128,512]{1,0:T(8,128)S(1)} %bitcast_select_fusion), channel_id=1, source_target_pairs={{1,0},{2,1},{3,2},{4,3},{5,4},{6,5},{7,6},{8,7},{9,8},{10,9},{11,1... | collective-permute-start | bytes 786440 | tf_op jit(solution)/shard_map/ppermute | solution.py:12
  70.2 9.9 %collective-permute-start.5 = (f32[128,512]{1,0:T(8,128)S(1)}, f32[128,512]{1,0:T(8,128)S(1)}, u32[]{:S(2)}, u32[]{:S(2)}) collective-permute-start(f32[128,512]{1,0:T(8,128)S(1)} %bitcast_select_fusion), channel_id=1, source_target_pairs={{2,0},{3,1},{4,2},{5,3},{6,4},{7,5},{8,6},{9,7},{10,8},{11,9},{12,... | collective-permute-start | bytes 786440 | tf_op jit(solution)/shard_map/ppermute | solution.py:12
  71.5 13.1 %collective-permute-start.6 = (f32[128,512]{1,0:T(8,128)S(1)}, f32[128,512]{1,0:T(8,128)S(1)}, u32[]{:S(2)}, u32[]{:S(2)}) collective-permute-start(f32[128,512]{1,0:T(8,128)S(1)} %bitcast_select_fusion), channel_id=1, source_target_pairs={{3,0},{4,1},{5,2},{6,3},{7,4},{8,5},{9,6},{10,7},{11,8},{12,9},{13... | collective-permute-start | bytes 786440 | tf_op jit(solution)/shard_map/ppermute | solution.py:12
  128.3 2.4 collective-permute-start.7
  130.7 8.3 %collective-permute-start.8 = (f32[128,512]{1,0:T(8,128)S(1)}, f32[128,512]{1,0:T(8,128)S(1)}, u32[]{:S(2)}, u32[]{:S(2)}) collective-permute-start(f32[128,512]{1,0:T(8,128)S(1)} %bitcast_select_fusion.1), channel_id=1, source_target_pairs={{1,0},{2,1},{3,2},{4,3},{5,4},{6,5},{7,6},{8,7},{9,8},{10,9},{11,1... | collective-permute-start | bytes 786440 | tf_op jit(solution)/shard_map/ppermute | solution.py:12
  132.7 10.1 %collective-permute-start.9 = (f32[128,512]{1,0:T(8,128)S(1)}, f32[128,512]{1,0:T(8,128)S(1)}, u32[]{:S(2)}, u32[]{:S(2)}) collective-permute-start(f32[128,512]{1,0:T(8,128)S(1)} %bitcast_select_fusion.1), channel_id=1, source_target_pairs={{2,0},{3,1},{4,2},{5,3},{6,4},{7,5},{8,6},{9,7},{10,8},{11,9},{12,... | collective-permute-start | bytes 786440 | tf_op jit(solution)/shard_map/ppermute | solution.py:12
  134.0 12.8 %collective-permute-start.10 = (f32[128,512]{1,0:T(8,128)S(1)}, f32[128,512]{1,0:T(8,128)S(1)}, u32[]{:S(2)}, u32[]{:S(2)}) collective-permute-start(f32[128,512]{1,0:T(8,128)S(1)} %bitcast_select_fusion.1), channel_id=1, source_target_pairs={{3,0},{4,1},{5,2},{6,3},{7,4},{8,5},{9,6},{10,7},{11,8},{12,9},{13... | collective-permute-start | bytes 786440 | tf_op jit(solution)/shard_map/ppermute | solution.py:12
  186.2 5.1 %collective-permute-start.11 = (f32[128,512]{1,0:T(8,128)S(1)}, f32[128,512]{1,0:T(8,128)S(1)}, u32[]{:S(2)}, u32[]{:S(2)}) collective-permute-start(f32[128,512]{1,0:T(8,128)S(1)} %broadcast_multiply_fusion.2), channel_id=1, source_target_pairs={{0,16},{16,32},{32,48},{48,64},{64,80},{80,96},{96,112},{112,128},... | collective-permute-start | bytes 786440 | tf_op jit(solution)/shard_map/ppermute | solution.py:12
  191.4 8.3 %collective-permute-start.12 = (f32[128,512]{1,0:T(8,128)S(1)}, f32[128,512]{1,0:T(8,128)S(1)}, u32[]{:S(2)}, u32[]{:S(2)}) collective-permute-start(f32[128,512]{1,0:T(8,128)S(1)} %bitcast_select_fusion.2), channel_id=1, source_target_pairs={{1,0},{2,1},{3,2},{4,3},{5,4},{6,5},{7,6},{8,7},{9,8},{10,9},{11,1... | collective-permute-start | bytes 786440 | tf_op jit(solution)/shard_map/ppermute | solution.py:12
  194.4 9.8 %collective-permute-start.13 = (f32[128,512]{1,0:T(8,128)S(1)}, f32[128,512]{1,0:T(8,128)S(1)}, u32[]{:S(2)}, u32[]{:S(2)}) collective-permute-start(f32[128,512]{1,0:T(8,128)S(1)} %bitcast_select_fusion.2), channel_id=1, source_target_pairs={{2,0},{3,1},{4,2},{5,3},{6,4},{7,5},{8,6},{9,7},{10,8},{11,9},{12,... | collective-permute-start | bytes 786440 | tf_op jit(solution)/shard_map/ppermute | solution.py:12
  195.7 11.7 %collective-permute-start.14 = (f32[128,512]{1,0:T(8,128)S(1)}, f32[128,512]{1,0:T(8,128)S(1)}, u32[]{:S(2)}, u32[]{:S(2)}) collective-permute-start(f32[128,512]{1,0:T(8,128)S(1)} %bitcast_select_fusion.2), channel_id=1, source_target_pairs={{3,0},{4,1},{5,2},{6,3},{7,4},{8,5},{9,6},{10,7},{11,8},{12,9},{13... | collective-permute-start | bytes 786440 | tf_op jit(solution)/shard_map/ppermute | solution.py:12
  247.8 11.3 %collective-permute-start.15 = (f32[128,512]{1,0:T(8,128)S(1)}, f32[128,512]{1,0:T(8,128)S(1)}, u32[]{:S(2)}, u32[]{:S(2)}) collective-permute-start(f32[128,512]{1,0:T(8,128)S(1)} %broadcast_multiply_fusion.1), channel_id=1, source_target_pairs={{0,16},{16,32},{32,48},{48,64},{64,80},{80,96},{96,112},{112,128},... | collective-permute-start | bytes 786440 | tf_op jit(solution)/shard_map/ppermute | solution.py:12
  259.1 8.3 %collective-permute-start.16 = (f32[128,512]{1,0:T(8,128)S(1)}, f32[128,512]{1,0:T(8,128)S(1)}, u32[]{:S(2)}, u32[]{:S(2)}) collective-permute-start(f32[128,512]{1,0:T(8,128)S(1)} %bitcast_select_fusion.3), channel_id=1, source_target_pairs={{1,0},{2,1},{3,2},{4,3},{5,4},{6,5},{7,6},{8,7},{9,8},{10,9},{11,1... | collective-permute-start | bytes 786440 | tf_op jit(solution)/shard_map/ppermute | solution.py:12
  262.5 9.8 %collective-permute-start.17 = (f32[128,512]{1,0:T(8,128)S(1)}, f32[128,512]{1,0:T(8,128)S(1)}, u32[]{:S(2)}, u32[]{:S(2)}) collective-permute-start(f32[128,512]{1,0:T(8,128)S(1)} %bitcast_select_fusion.3), channel_id=1, source_target_pairs={{2,0},{3,1},{4,2},{5,3},{6,4},{7,5},{8,6},{9,7},{10,8},{11,9},{12,... | collective-permute-start | bytes 786440 | tf_op jit(solution)/shard_map/ppermute | solution.py:12
  263.8 11.3 %collective-permute-start.18 = (f32[128,512]{1,0:T(8,128)S(1)}, f32[128,512]{1,0:T(8,128)S(1)}, u32[]{:S(2)}, u32[]{:S(2)}) collective-permute-start(f32[128,512]{1,0:T(8,128)S(1)} %bitcast_select_fusion.3), channel_id=1, source_target_pairs={{3,0},{4,1},{5,2},{6,3},{7,4},{8,5},{9,6},{10,7},{11,8},{12,9},{13... | collective-permute-start | bytes 786440 | tf_op jit(solution)/shard_map/ppermute | solution.py:12
  279.9 105.0 %copy-start.1 = (f32[1,128]{1,0:T(1,128)S(1)}, f32[1,128]{1,0:T(1,128)}, u32[]{:S(2)}) copy-start(f32[1,128]{1,0:T(1,128)} %param.8) | copy-start | bytes 1540
  315.9 12.7 %collective-permute-start.19 = (f32[128,512]{1,0:T(8,128)S(1)}, f32[128,512]{1,0:T(8,128)S(1)}, u32[]{:S(2)}, u32[]{:S(2)}) collective-permute-start(f32[128,512]{1,0:T(8,128)S(1)} %broadcast_multiply_fusion), channel_id=1, source_target_pairs={{0,16},{16,32},{32,48},{48,64},{64,80},{80,96},{96,112},{112,128},... | collective-permute-start | bytes 786440 | tf_op jit(solution)/shard_map/ppermute | solution.py:12
  328.7 8.3 %collective-permute-start.20 = (f32[128,512]{1,0:T(8,128)S(1)}, f32[128,512]{1,0:T(8,128)S(1)}, u32[]{:S(2)}, u32[]{:S(2)}) collective-permute-start(f32[128,512]{1,0:T(8,128)S(1)} %bitcast_select_fusion.4), channel_id=1, source_target_pairs={{1,0},{2,1},{3,2},{4,3},{5,4},{6,5},{7,6},{8,7},{9,8},{10,9},{11,1... | collective-permute-start | bytes 786440 | tf_op jit(solution)/shard_map/ppermute | solution.py:12
  331.7 9.8 %collective-permute-start.21 = (f32[128,512]{1,0:T(8,128)S(1)}, f32[128,512]{1,0:T(8,128)S(1)}, u32[]{:S(2)}, u32[]{:S(2)}) collective-permute-start(f32[128,512]{1,0:T(8,128)S(1)} %bitcast_select_fusion.4), channel_id=1, source_target_pairs={{2,0},{3,1},{4,2},{5,3},{6,4},{7,5},{8,6},{9,7},{10,8},{11,9},{12,... | collective-permute-start | bytes 786440 | tf_op jit(solution)/shard_map/ppermute | solution.py:12
  333.0 11.7 %collective-permute-start.22 = (f32[128,512]{1,0:T(8,128)S(1)}, f32[128,512]{1,0:T(8,128)S(1)}, u32[]{:S(2)}, u32[]{:S(2)}) collective-permute-start(f32[128,512]{1,0:T(8,128)S(1)} %bitcast_select_fusion.4), channel_id=1, source_target_pairs={{3,0},{4,1},{5,2},{6,3},{7,4},{8,5},{9,6},{10,7},{11,8},{12,9},{13... | collective-permute-start | bytes 786440 | tf_op jit(solution)/shard_map/ppermute | solution.py:12
  385.0 10.9 %collective-permute-start.23 = (f32[128]{0:T(128)S(1)}, f32[128]{0:T(128)S(1)}, u32[]{:S(2)}, u32[]{:S(2)}) collective-permute-start(f32[128]{0:T(128)S(1)} %fusion.88), channel_id=1, source_target_pairs={{0,16},{16,32},{32,48},{48,64},{64,80},{80,96},{96,112},{112,128},... | collective-permute-start | bytes 1544 | tf_op jit(solution)/shard_map/ppermute | solution.py:12
  395.9 15.6 %collective-permute-start.24 = (f32[128]{0:T(128)S(1)}, f32[128]{0:T(128)S(1)}, u32[]{:S(2)}, u32[]{:S(2)}) collective-permute-start(f32[128]{0:T(128)S(1)} %fusion.79), channel_id=1, source_target_pairs={{0,16},{16,32},{32,48},{48,64},{64,80},{80,96},{96,112},{112,128},... | collective-permute-start | bytes 1544 | tf_op jit(solution)/shard_map/ppermute | solution.py:12
  411.5 4.9 %collective-permute-start.25 = (f32[128]{0:T(128)S(1)}, f32[128]{0:T(128)S(1)}, u32[]{:S(2)}, u32[]{:S(2)}) collective-permute-start(f32[128]{0:T(128)S(1)} %fusion.81), channel_id=1, source_target_pairs={{0,16},{16,32},{32,48},{48,64},{64,80},{80,96},{96,112},{112,128},... | collective-permute-start | bytes 1544 | tf_op jit(solution)/shard_map/ppermute | solution.py:12
  416.4 4.9 %collective-permute-start.26 = (f32[128]{0:T(128)S(1)}, f32[128]{0:T(128)S(1)}, u32[]{:S(2)}, u32[]{:S(2)}) collective-permute-start(f32[128]{0:T(128)S(1)} %fusion.83), channel_id=1, source_target_pairs={{0,16},{16,32},{32,48},{48,64},{64,80},{80,96},{96,112},{112,128},... | collective-permute-start | bytes 1544 | tf_op jit(solution)/shard_map/ppermute | solution.py:12
  421.3 4.9 %collective-permute-start.27 = (f32[128]{0:T(128)S(1)}, f32[128]{0:T(128)S(1)}, u32[]{:S(2)}, u32[]{:S(2)}) collective-permute-start(f32[128]{0:T(128)S(1)} %fusion.85), channel_id=1, source_target_pairs={{0,16},{16,32},{32,48},{48,64},{64,80},{80,96},{96,112},{112,128},... | collective-permute-start | bytes 1544 | tf_op jit(solution)/shard_map/ppermute | solution.py:12
where the time goes:
time: 434 us; the launch traced here: 427 us
  blocking collectives  218 us (50%)
  starting transfers between devices  100 us (23%)
  waiting for transfers between devices  76.4 us (18%)
  matrix products  29.1 us (7%)
    psum x6, blocking collectives, step_now(): picked_sum, total_sum = lax.psum((picked_part, total_part), 'sector')  218 us
    ppermute x28, starting transfers between devices, passed_along(): lax.ppermute(value, axis, [(source, source + steps) for source in range(i...  100 us
    ppermute x28, waiting for transfers between devices, passed_along(): lax.ppermute(value, axis, [(source, source + steps) for source in range(i...  76.4 us
    dot_general x6, matrix products, sector_products(): jnp.einsum('rnsi,nsij->rnsj', stacked, weights, precision=lax.Precision.H...  29.1 us
  transfers between devices with their start and end apart: 28, of which 28 were waited for; matrix products, arithmetic and copies ran while one was open for 0% of the time, Pallas kernels for 0%

commit v1 on v0

v1 whole, which is shorter than its diff:
```python
import functools

import jax
import jax.numpy as jnp
from jax import lax
from jax.experimental import pallas as pl
from jax.experimental.pallas import tpu as pltpu
from jax.sharding import PartitionSpec as P

EPSILON = 1e-06
CHUNKS = 4
LANES = 128
MESH = pl.DeviceIdType.MESH


def when(condition):
    return pl.when(condition)


def lane_and_row(rows):
    lane = lax.broadcasted_iota(jnp.int32, (rows, LANES), 1)
    row = lax.broadcasted_iota(jnp.int32, (rows, LANES), 0)
    return lane, row


def column_of(vector, offset, rows):
    lane, row = lane_and_row(rows)
    spread = jnp.broadcast_to(vector, (rows, LANES))
    return jnp.sum(jnp.where(lane == row + offset, spread, 0.0), axis=1, keepdims=True)


def vector_of(columns, rows):
    lane, row = lane_and_row(rows)
    spread = jnp.zeros((rows, LANES), jnp.float32)
    for offset, column in columns:
        spread = spread + jnp.where(lane == row + offset, column, 0.0)
    return jnp.sum(spread, axis=0, keepdims=True)


def halves(value):
    high = value.astype(jnp.bfloat16)
    return high, (value - high.astype(jnp.float32)).astype(jnp.bfloat16)


def kernel(
    ticks,
    side,
    sites,
    bond,
    site_tensor,
    outcomes,
    in_flight,
    prior,
    entering,
    env_out,
    logp_out,
    raw,
    high,
    low,
    slots,
    picked,
    message,
    along_x,
    along_y,
    raw_sem,
    local_sem,
    slot_sem,
    x_sem,
    y_sem,
    send_sem,
    x_send_sem,
    y_send_sem,
):
    site, sector = lax.axis_index("site"), lax.axis_index("sector")
    x, y = sector % side, sector // side
    sectors = side * side
    last = sectors - 1
    rows = slots.shape[3]

    def local_row(index):
        return pltpu.make_async_copy(
            in_flight.at[0, pl.ds(index * rows, rows), :], slots.at[0, index, 0], slot_sem.at[0, index, 0]
        )

    def local_entering(tick, index):
        return pltpu.make_async_copy(
            entering.at[tick - 1, pl.ds(index * rows, rows), :],
            slots.at[tick, index, 0],
            slot_sem.at[tick, index, 0],
        )

    raw_copies = [
        pltpu.make_async_copy(site_tensor.at[0, count, 0], raw.at[count], raw_sem.at[count]) for count in range(4)
    ]
    for index in range(CHUNKS):
        local_row(index).start()
    for copy in raw_copies:
        copy.start()

    for count in range(1, 4):

        @when(sector + count > last)
        def _():
            def clear(index, carry):
                slots[index // CHUNKS, index % CHUNKS, count] = jnp.zeros((rows, slots.shape[4]), jnp.float32)
                return carry

            lax.fori_loop(0, ticks * CHUNKS, clear, 0)

    along_x[...] = jnp.zeros_like(along_x)
    along_y[...] = jnp.zeros_like(along_y)

    barrier = pltpu.get_barrier_semaphore()

    def greet(condition, where):
        @when(condition)
        def _():
            pl.semaphore_signal(barrier, inc=1, device_id=where, device_id_type=MESH)

    always = site >= 0
    expected = jnp.int32(2 * (side - 1))
    for hop in range(1, side):
        greet(always, (site, y * side + (x + hop) % side))
        greet(always, (site, (y + hop) % side * side + x))
    greet((x == side - 1) & (sector < last), (site, sector + 1))
    expected += ((x == 0) & (sector > 0)).astype(jnp.int32)
    greet((x != 0) & (sector + 3 <= last), (site, sector + 3))
    expected += ((x != side - 1) & (sector >= 3)).astype(jnp.int32)
    greet((x == 0) & (sector > 0), (site, sector - 1))
    expected += ((x == side - 1) & (sector < last)).astype(jnp.int32)
    has_next = site < sites - 1
    for hop in range(side):
        greet(site > 0, (site - 1, y * side + (x + hop) % side))
        expected += has_next.astype(jnp.int32)
    greet((site > 0) & (x == side - 1) & (sector < last), (site - 1, sector + 1))
    expected += (has_next & (x == 0) & (sector > 0)).astype(jnp.int32)
    greet((site > 0) & (x != 0) & (sector + 3 <= last), (site - 1, sector + 3))
    expected += (has_next & (x != side - 1) & (sector >= 3)).astype(jnp.int32)
    pl.semaphore_wait(barrier, expected)

    def remote(source, tick, index, count, kind, where):
        return pltpu.make_async_remote_copy(
            src_ref=source,
            dst_ref=slots.at[tick, index, count],
            send_sem=send_sem.at[kind, tick, index],
            recv_sem=slot_sem.at[tick, index, count],
            device_id=where,
            device_id_type=MESH,
        )

    def first_sends(index):
        source = in_flight.at[0, pl.ds(index * rows, rows), :]
        return [
            (sector >= 1, remote(source, 0, index, 1, 0, (site, sector - 1))),
            (sector >= 3, remote(source, 0, index, 3, 1, (site, sector - 3))),
        ]

    def next_sends(tick, index):
        source = picked.at[tick, index]
        return [
            (has_next & (sector >= 1), remote(source, tick + 1, index, 1, 0, (site + 1, sector - 1))),
            (has_next & (sector >= 3), remote(source, tick + 1, index, 3, 1, (site + 1, sector - 3))),
            (has_next, remote(source, tick + 1, index, 0, 2, (site + 1, sector))),
        ]

    def entering_sends(tick, index):
        source = entering.at[tick, pl.ds(index * rows, rows), :]
        return [
            ((site == 0) & (sector >= 1), remote(source, tick + 1, index, 1, 3, (site, sector - 1))),
            ((site == 0) & (sector >= 3), remote(source, tick + 1, index, 3, 4, (site, sector - 3))),
        ]

    def by_left(of_sector):
        return (of_sector == 2) | ((site % 2 == 0) & (of_sector % side != 1))

    def relays(tick, index):
        one, three = sector + 1, sector + 3
        return [
            (
                (one <= last) & (sector >= 1) & by_left(one),
                remote(slots.at[tick, index, 1], tick, index, 2, 5, (site, sector - 1)),
            ),
            (
                (three <= last) & jnp.logical_not(by_left(three)),
                remote(slots.at[tick, index, 3], tick, index, 2, 6, (site, sector + 1)),
            ),
        ]

    def start(copies):
        for condition, copy in copies:
            when(condition)(copy.start)

    def finish(copies):
        for condition, copy in copies:
            when(condition)(copy.wait_send)

    def arrived(tick, index, count):
        remote(slots.at[tick, index, count], tick, index, count, 0, (site, sector)).wait_recv()

    def x_sends(tick, index, to_site):
        return [
            pltpu.make_async_remote_copy(
                src_ref=message.at[tick, index],
                dst_ref=along_x.at[tick + 1, index, x],
                send_sem=x_send_sem.at[tick, index],
                recv_sem=x_sem.at[tick + 1, index],
                device_id=(to_site, y * side + (x + hop) % side),
                device_id_type=MESH,
            )
            for hop in range(side)
        ]

    def y_sends(tick, index):
        return [
            pltpu.make_async_remote_copy(
                src_ref=along_y.at[tick, index, y],
                dst_ref=along_y.at[tick, index, y],
                send_sem=y_send_sem.at[tick, index],
                recv_sem=y_sem.at[tick, index],
                device_id=(site, (y + hop) % side * side + x),
                device_id_type=MESH,
            )
            for hop in range(1, side)
        ]

    def four(ref, tick, index):
        return (ref[tick, index, 0] + ref[tick, index, 1]) + (ref[tick, index, 2] + ref[tick, index, 3])

    def sums_to_rows(tick, index, parts):
        group = along_x.at[tick, index, pl.ds(0, parts)]
        pltpu.make_async_copy(group, group, x_sem.at[tick, index]).wait()
        along_y[tick, index, y] = four(along_x, tick, index)
        for copy in y_sends(tick, index):
            copy.start()

    def sums_arrived(tick, index):
        group = along_y.at[tick, index, pl.ds(0, side - 1)]
        pltpu.make_async_copy(group, group, y_sem.at[tick, index]).wait()

    def sums_of(tick, index):
        total = four(along_y, tick, index)
        picked_power = column_of(total, 0, rows) / bond + EPSILON
        total_power = column_of(total, rows, rows) / bond + EPSILON
        log_weight = column_of(total, 2 * rows, rows) / sectors
        scale = 1.0 / jnp.sqrt(picked_power)
        return scale, log_weight + jnp.log(picked_power) - jnp.log(total_power)

    def pass_on(tick, index):
        @when((tick > 0) & (site > 0))
        def _():
            sums_to_rows(tick, index, side)

        @when(sector + 1 <= last)
        def _():
            arrived(tick, index, 1)

        (left_condition, left), (right_condition, right) = relays(tick, index)
        when(left_condition)(left.start)

        @when(sector + 3 <= last)
        def _():
            arrived(tick, index, 3)

        when(right_condition)(right.start)

    def work(tick, index):
        is_first, is_entering = tick == 0, site == 0

        @when(is_first | is_entering)
        def _():
            pltpu.make_async_copy(slots.at[tick, index, 0], slots.at[tick, index, 0], slot_sem.at[tick, index, 0]).wait()

        @when(jnp.logical_not(is_first | is_entering))
        def _():
            arrived(tick, index, 0)
            sums_arrived(tick, index)

        @when(sector + 2 <= last)
        def _():
            arrived(tick, index, 2)

        products = []
        for count in range(4):
            block_high, block_low = halves(slots[tick, index, count])
            both = jnp.dot(
                jnp.concatenate([block_high, block_low], axis=0), high[count], preferred_element_type=jnp.float32
            )
            rest = jnp.dot(block_high, low[count], preferred_element_type=jnp.float32)
            products.append(both[:rows] + (both[rows:] + rest))
        scale, log_weight = sums_of(tick, index)
        fresh = is_first | is_entering
        scale = jnp.where(fresh, 1.0, scale)
        own_prior = jnp.where(is_first, column_of(prior[...], index * rows, rows), 0.0)
        log_weight = jnp.where(fresh, own_prior, log_weight)
        chosen = column_of(outcomes[tick].astype(jnp.float32), index * rows, rows)
        selected = jnp.zeros_like(products[0])
        squares = jnp.zeros_like(products[0])
        for count in range(4):
            amplitude = products[count] * scale
            selected = jnp.where(chosen == float(count), amplitude, selected)
            squares = squares + amplitude * amplitude
        picked[tick, index] = selected
        message[tick, index] = vector_of(
            [
                (0, jnp.sum(selected * selected, axis=1, keepdims=True)),
                (rows, jnp.sum(squares, axis=1, keepdims=True)),
                (2 * rows, log_weight),
            ],
            rows,
        )

        @when(tick < ticks - 1)
        def _():
            @when(has_next)
            def _():
                for copy in x_sends(tick, index, site + 1):
                    copy.start()

            start(next_sends(tick, index))
            start(entering_sends(tick, index))

        @when(tick == ticks - 1)
        def _():
            for copy in x_sends(tick, index, site)[1:]:
                copy.start()
            along_x[ticks, index, x] = message[tick, index]

    for index in range(CHUNKS):
        start(first_sends(index))

    @when(site == 0)
    def _():
        for tick in range(1, ticks):
            for index in range(CHUNKS):
                local_entering(tick, index).start()

    for count in range(4):
        raw_copies[count].wait()

        def cut(step, carry):
            part = pl.ds(pl.multiple_of(step * 64, 64), 64)
            high[count, part, :], low[count, part, :] = halves(raw[count, part, :])
            return carry

        lax.fori_loop(0, raw.shape[1] // 64, cut, 0)

    steps = ticks * CHUNKS
    pass_on(0, 0)

    def step(number, carry):
        @when(number + 1 < steps)
        def _():
            pass_on((number + 1) // CHUNKS, (number + 1) % CHUNKS)

        work(number // CHUNKS, number % CHUNKS)
        return carry

    lax.fori_loop(0, steps, step, 0)

    for index in range(CHUNKS):
        sums_to_rows(ticks, index, side - 1)
    final = jnp.zeros((1, LANES), jnp.float32)
    for index in range(CHUNKS):
        sums_arrived(ticks, index)
        scale, log_weight = sums_of(ticks, index)
        env_out[0, index * rows : (index + 1) * rows, :] = picked[ticks - 1, index] * scale
        final = final + vector_of([(index * rows, log_weight)], rows)
    logp_out[...] = final

    def drain(number, carry):
        tick, index = number // CHUNKS, number % CHUNKS
        finish(relays(tick, index))

        @when(tick < ticks - 1)
        def _():
            finish(next_sends(tick, index))
            finish(entering_sends(tick, index))

        parts = jnp.where(tick < ticks - 1, side, side - 1)

        @when((tick < ticks - 1) & has_next)
        def _():
            group = along_x.at[0, 0]
            pltpu.make_async_copy(group, group, x_send_sem.at[tick, index]).wait()

        @when(tick == ticks - 1)
        def _():
            group = along_x.at[0, 0, pl.ds(0, side - 1)]
            pltpu.make_async_copy(group, group, x_send_sem.at[tick, index]).wait()

        @when((tick > 0) & (site > 0))
        def _():
            group = along_y.at[0, 0, pl.ds(0, side - 1)]
            pltpu.make_async_copy(group, group, y_send_sem.at[tick, index]).wait()

        return carry

    lax.fori_loop(0, steps, drain, 0)
    for index in range(CHUNKS):
        finish(first_sends(index))
        group = along_y.at[0, 0, pl.ds(0, side - 1)]
        pltpu.make_async_copy(group, group, y_send_sem.at[ticks, index]).wait()


def solution(mesh):
    sites, sectors = mesh.shape["site"], mesh.shape["sector"]
    side = int(round(sectors**0.5))

    def per_device(site_tensor, outcomes, in_flight, prior_logp, entering):
        ticks = outcomes.shape[0]
        _, counts, _, width, _ = site_tensor.shape
        rows = in_flight.shape[1] // CHUNKS
        anywhere = pl.BlockSpec(memory_space=pl.ANY)
        vmem = pl.BlockSpec(memory_space=pltpu.VMEM)
        f32, dma = jnp.float32, pltpu.SemaphoreType.DMA
        return pl.pallas_call(
            functools.partial(kernel, ticks, side, sites, float(width * sectors)),
            name="chain",
            out_shape=(
                jax.ShapeDtypeStruct(in_flight.shape, f32),
                jax.ShapeDtypeStruct(prior_logp.shape, f32),
            ),
            in_specs=[anywhere, vmem, anywhere, vmem, anywhere],
            out_specs=(vmem, vmem),
            scratch_shapes=[
                pltpu.VMEM((counts, width, width), f32),
                pltpu.VMEM((counts, width, width), jnp.bfloat16),
                pltpu.VMEM((counts, width, width), jnp.bfloat16),
                pltpu.VMEM((ticks, CHUNKS, counts, rows, width), f32),
                pltpu.VMEM((ticks, CHUNKS, rows, width), f32),
                pltpu.VMEM((ticks, CHUNKS, 1, LANES), f32),
                pltpu.VMEM((ticks + 1, CHUNKS, side, 1, LANES), f32),
                pltpu.VMEM((ticks + 1, CHUNKS, side, 1, LANES), f32),
                dma((counts,)),
                dma((1,)),
                dma((ticks, CHUNKS, counts)),
                dma((ticks + 1, CHUNKS)),
                dma((ticks + 1, CHUNKS)),
                dma((7, ticks, CHUNKS)),
                dma((ticks, CHUNKS)),
                dma((ticks + 1, CHUNKS)),
            ],
            compiler_params=pltpu.CompilerParams(
                collective_id=0, has_side_effects=True, vmem_limit_bytes=48 * 1024 * 1024
            ),
            cost_estimate=pl.CostEstimate(
                flops=6 * ticks * counts * rows * CHUNKS * width * width,
                bytes_accessed=4 * counts * width * width,
                transcendentals=0,
            ),
        )(site_tensor, outcomes, in_flight, prior_logp, entering)

    return jax.shard_map(
        per_device,
        mesh=mesh,
        in_specs=(
            P("site", None, "sector", None, None),
            P(None, "site", None),
            P("site", None, "sector"),
            P("site", None),
            P(None, None, "sector"),
        ),
        out_specs=(P("site", None, "sector"), P("site", None)),
        check_vma=False,
    )
```

time: 434 us -> 119 us (0.27)
  the two profiles are of different devices: /device:TPU:2 before, /device:TPU:32 now
where the time goes in v1:
time: 119 us
  Pallas kernels  111 us (93%)
  local copies, waits for them, and re-layouts  7 us (6%)
    pallas_call x1, Pallas kernels, per_device(): pl.pallas_call(functools.partial(kernel, ticks, side, sites, float(width...  111 us
    unnamed x12, local copies, waits for them, and re-layouts  7 us

profile of v1, /device:TPU:32, one launch (start us, length us, event | category | flops | bytes accessed | tf_op | source)
XLA Modules:
  0.0 118.9 jit_solution(1176139237181063)
XLA Ops:
  0.6 0.0 copy-start
  0.6 2.2 %copy-done = f32[1,4,1,512,512]{4,3,2,1,0:T(8,128)S(1)} copy-done((f32[1,4,1,512,512]{4,3,2,1,0:T(8,128)S(1)}, f32[1,4,1,512,512]{4,3,2,1,0:T(8,128)}, u32[]{:S(2)}) %copy-start) | copy-done | bytes 4194328
  2.8 0.0 copy-start.1
  2.8 1.3 %copy-done.1 = f32[5,128,512]{2,1,0:T(8,128)S(1)} copy-done((f32[5,128,512]{2,1,0:T(8,128)S(1)}, f32[5,128,512]{2,1,0:T(8,128)}, u32[]{:S(2)}) %copy-start.1) | copy-done | bytes 1310744
  4.1 0.0 copy-start.2
  4.1 0.9 copy-done.2
  5.1 0.0 copy-start.3
  5.1 0.7 copy-done.3
  5.8 0.0 copy-start.4
  5.8 0.7 copy-done.4
  6.4 111.2 %chain.1 = (f32[1,128,512]{2,1,0:T(8,128)S(1)}, f32[1,128]{1,0:T(1,128)S(1)}) custom-call(f32[1,4,1,512,512]{4,3,2,1,0:T(8,128)S(1)} %copy-done, s32[6,1,128]{2,1,0:T(1,128)S(1)} %copy-done.3, f32[1,128,512]{2,1,0:T(8,128)S(1)} %copy-done.2, f32[1,128]{1,0:T(1,128)S(1)} %copy-done.4, f32[5,128,512]{2,1,0:T(8,128)S(1)} %copy-done.1), custom_call_target="tpu_custom_call" | custom-call | flops 4831838208 | bytes 4194304 | tf_op jit(solution)/shard_map/chain/pallas_call | solution.py:416
  117.7 0.7 copy.9
  118.4 0.5 copy.10
Async XLA Ops:
  0.6 2.2 %copy-start = (f32[1,4,1,512,512]{4,3,2,1,0:T(8,128)S(1)}, f32[1,4,1,512,512]{4,3,2,1,0:T(8,128)}, u32[]{:S(2)}) copy-start(f32[1,4,1,512,512]{4,3,2,1,0:T(8,128)} %site_tensor.1) | copy-start | bytes 12582916
  2.8 1.3 %copy-start.1 = (f32[5,128,512]{2,1,0:T(8,128)S(1)}, f32[5,128,512]{2,1,0:T(8,128)}, u32[]{:S(2)}) copy-start(f32[5,128,512]{2,1,0:T(8,128)} %entering.1) | copy-start | bytes 3932164
  4.1 0.9 copy-start.2
  5.1 0.7 copy-start.3
  5.8 0.7 copy-start.4

commit v2 on v1

v2 whole, which is shorter than its diff:
```python
import functools

import jax
import jax.numpy as jnp
from jax import lax
from jax.experimental import pallas as pl
from jax.experimental.pallas import tpu as pltpu
from jax.sharding import PartitionSpec as P

EPSILON = 1e-06
CHUNKS = 4
AHEAD = 2
LANES = 128
MESH = pl.DeviceIdType.MESH


def when(condition):
    return pl.when(condition)


def diagonal():
    lane = lax.broadcasted_iota(jnp.int32, (LANES, LANES), 1)
    row = lax.broadcasted_iota(jnp.int32, (LANES, LANES), 0)
    return lane == row


def column_of(vector):
    spread = jnp.where(diagonal(), jnp.broadcast_to(vector, (LANES, LANES)), 0.0)
    return jnp.broadcast_to(jnp.sum(spread, axis=1, keepdims=True), (LANES, LANES))


def sums_of_rows(value):
    spread = jnp.where(diagonal(), jnp.sum(value, axis=1, keepdims=True), 0.0)
    return jnp.sum(spread, axis=0, keepdims=True)


def halves(value):
    high = value.astype(jnp.bfloat16)
    return high, (value - high.astype(jnp.float32)).astype(jnp.bfloat16)


def kernel(
    ticks,
    side,
    sites,
    bond,
    site_tensor,
    outcomes_in,
    in_flight,
    prior_in,
    entering,
    env_out,
    logp_out,
    outcomes,
    prior,
    raw,
    high,
    low,
    slots,
    picked,
    chosen,
    scale,
    picked_fold,
    total_fold,
    carried,
    message,
    along_x,
    along_y,
    raw_sem,
    local_sem,
    slot_sem,
    x_sem,
    y_sem,
    send_sem,
    x_send_sem,
    y_send_sem,
):
    site, sector = lax.axis_index("site"), lax.axis_index("sector")
    x, y = sector % side, sector // side
    last = side * side - 1
    last_site = sites - 1
    next_site = (site + 1) % sites
    site_before = (site + sites - 1) % sites
    even = site % 2 == 0
    rows = slots.shape[3]
    width = slots.shape[4]
    tiles = width // LANES
    always = site >= 0

    raw_copies = [
        pltpu.make_async_copy(site_tensor.at[0, count, 0], raw.at[count], raw_sem.at[count]) for count in range(4)
    ]
    small_copies = [
        pltpu.make_async_copy(outcomes_in, outcomes, local_sem.at[0]),
        pltpu.make_async_copy(prior_in, prior, local_sem.at[1]),
    ]
    row_copies = [
        pltpu.make_async_copy(
            in_flight.at[0, pl.ds(index * rows, rows), :], slots.at[0, index, 0], slot_sem.at[0, index, 0]
        )
        for index in range(CHUNKS)
    ]

    def entering_copy(tick, index):
        return pltpu.make_async_copy(
            entering.at[tick, pl.ds(index * rows, rows), :], picked.at[tick, index], local_sem.at[2 + tick * CHUNKS + index]
        )

    barrier = pltpu.get_barrier_semaphore()
    expected = jnp.int32(0)

    def greet(from_condition, where, to_condition):
        @when(from_condition)
        def _():
            pl.semaphore_signal(barrier, inc=1, device_id=where, device_id_type=MESH)

        return to_condition.astype(jnp.int32)

    for near, own in ((site, False), (site_before, True)):
        for hop in range(0 if own else 1, side):
            expected += greet(always, (near, y * side + (x + hop) % side), always)
        for hop in range(1, side):
            expected += greet(always, (near, (y + hop) % side * side + x), always)
        expected += greet((x == side - 1) & (sector < last), (near, sector + 1), (x == 0) & (sector > 0))
        expected += greet((x != 0) & (sector + 3 <= last), (near, sector + 3), (x != side - 1) & (sector >= 3))
    expected += greet((x == 0) & (sector > 0), (site, sector - 1), (x == side - 1) & (sector < last))

    for copy in row_copies + small_copies + raw_copies:
        copy.start()

    pl.semaphore_wait(barrier, expected)

    def remote(source, tick, index, count, kind, where):
        return pltpu.make_async_remote_copy(
            src_ref=source,
            dst_ref=slots.at[tick, index, count],
            send_sem=send_sem.at[kind, tick, index],
            recv_sem=slot_sem.at[tick, index, count],
            device_id=where,
            device_id_type=MESH,
        )

    odd_to = next_site % 2 == 1

    def sends(source, tick, index, to_site, odd):
        first_column = odd & (x == 0)
        third_column = odd & (x == 2)
        return [
            ((sector >= 1) & jnp.logical_not(first_column), remote(source, tick, index, 1, 0, (to_site, sector - 1))),
            ((sector >= 3) & jnp.logical_not(third_column), remote(source, tick, index, 3, 1, (to_site, sector - 3))),
            ((sector >= side) & (first_column | third_column), remote(source, tick, index, 4, 2, (to_site, sector - side))),
            ((sector == 2) & jnp.logical_not(odd), remote(source, tick, index, 4, 2, (to_site, sector + 1))),
        ]

    def first_sends(index):
        return sends(in_flight.at[0, pl.ds(index * rows, rows), :], 0, index, site, jnp.logical_not(even))

    def next_sends(tick, index):
        source = picked.at[tick, index]
        own = (always, remote(source, tick + 1, index, 0, 3, (next_site, sector)))
        return sends(source, tick + 1, index, next_site, odd_to) + [own]

    def by_left(of_sector):
        return even == (of_sector % side < 2)

    left_on = (sector + 1 <= last) & (sector >= 1) & by_left(sector + 1)
    right_on = (sector + 3 <= last) & jnp.logical_not(by_left(sector + 3))
    crossed = jnp.logical_not(even) & (sector + side <= last)
    stage_first, stage_third = crossed & (x == 0), crossed & (x == 2)
    stage_two = even & (sector == 3)

    def relays(tick, index):
        stage, one, three = slots.at[tick, index, 4], slots.at[tick, index, 1], slots.at[tick, index, 3]
        return [
            (stage_first, 4, remote(stage, tick, index, 1, 4, (site, sector + 3))),
            (stage_third, 4, remote(stage, tick, index, 3, 4, (site, sector + 1))),
            (stage_two, 4, remote(stage, tick, index, 2, 4, (site, sector - 3))),
            (left_on, 1, remote(one, tick, index, 2, 5, (site, sector - 1))),
            (right_on, 3, remote(three, tick, index, 2, 6, (site, sector + 1))),
        ]

    def start(copies):
        for condition, copy in copies:
            when(condition)(copy.start)

    def finish(copies):
        for condition, copy in copies:
            when(condition)(copy.wait_send)

    def arrived(tick, index, count):
        remote(slots.at[tick, index, count], tick, index, count, 0, (site, sector)).wait_recv()

    def x_sends(tick, to_site):
        return [
            pltpu.make_async_remote_copy(
                src_ref=message.at[tick],
                dst_ref=along_x.at[tick + 1, x],
                send_sem=x_send_sem.at[tick],
                recv_sem=x_sem.at[tick + 1],
                device_id=(to_site, y * side + (x + hop) % side),
                device_id_type=MESH,
            )
            for hop in range(side)
        ]

    def y_sends(slot, to_site):
        return [
            pltpu.make_async_remote_copy(
                src_ref=carried.at[slot],
                dst_ref=along_y.at[slot, y],
                send_sem=y_send_sem.at[slot],
                recv_sem=y_sem.at[slot],
                device_id=(to_site, (y + hop) % side * side + x),
                device_id_type=MESH,
            )
            for hop in range(side)
        ]

    def wait_for(ref, sem):
        pltpu.make_async_copy(ref, ref, sem).wait()

    def four(ref, tick):
        return (ref[tick, 0] + ref[tick, 1]) + (ref[tick, 2] + ref[tick, 3])

    def advance(slot):
        sums = four(along_y, slot)
        before = along_y[slot, 0]
        before_log, before_scale = before[2:3], before[3:4]
        picked_power = sums[0:1] * before_scale * before_scale / bond + EPSILON
        total_power = sums[1:2] * before_scale * before_scale / bond + EPSILON
        return 1.0 / jnp.sqrt(picked_power), before_log + jnp.log(picked_power) - jnp.log(total_power)

    def age_at(tick):
        return jnp.minimum(tick, site)

    def begin(tick):
        age = age_at(tick)

        @when(age >= 2)
        def _():
            wait_for(along_y.at[tick], y_sem.at[tick])
            now_scale, now_log = advance(tick)
            carried[tick + 1, 2:3, :] = now_log
            carried[tick + 1, 3:4, :] = now_scale
            scale[...] = column_of(now_scale)

        @when(age < 2)
        def _():
            carried[tick + 1, 2:3, :] = jnp.where(tick == 0, prior[...], 0.0)
            carried[tick + 1, 3:4, :] = jnp.ones((1, LANES), jnp.float32)
            scale[...] = jnp.ones_like(scale)

    def middle(tick):
        @when(age_at(tick) >= 1)
        def _():
            wait_for(along_x.at[tick], x_sem.at[tick])
            sums = four(along_x, tick)
            carried[tick + 1, 0:2, :] = sums[0:2]

            @when(age_at(tick) == 1)
            def _():
                carried[tick + 1, 2:3, :] = along_x[tick, 0][2:3]

            @when((tick < ticks - 1) & (site < last_site))
            def _():
                for copy in y_sends(tick + 1, next_site):
                    copy.start()

            @when(tick == ticks - 1)
            def _():
                for copy in y_sends(ticks, site)[1:]:
                    copy.start()
                along_y[ticks, y] = carried[ticks]

    def end(tick):
        message[tick, 0:1, :] = sums_of_rows(picked_fold[...])
        message[tick, 1:2, :] = sums_of_rows(total_fold[...])
        message[tick, 2:3, :] = carried[tick + 1, 2:3, :]
        message[tick, 3:4, :] = carried[tick + 1, 3:4, :]

        @when((tick < ticks - 1) & (site < last_site))
        def _():
            for copy in x_sends(tick, next_site):
                copy.start()

        @when(tick == ticks - 1)
        def _():
            for copy in x_sends(tick, site)[1:]:
                copy.start()
            along_x[ticks, x] = message[ticks - 1]

    def pass_on(tick, index):
        for condition, count, copy in relays(tick, index):

            @when(condition)
            def _():
                arrived(tick, index, count)
                copy.start()

    def work(tick, index, meanwhile):
        @when(tick == 0)
        def _():
            wait_for(slots.at[0, index, 0], slot_sem.at[0, index, 0])

        @when(tick > 0)
        def _():
            arrived(tick, index, 0)

        part = pl.ds(pl.multiple_of(index * rows, rows), rows)
        factor = jnp.concatenate([scale[part, :]] * tiles, axis=1)
        choice = jnp.concatenate([chosen[tick, part, :]] * tiles, axis=1)
        selected = jnp.zeros((rows, width), jnp.float32)
        squares = jnp.zeros((rows, width), jnp.float32)
        for count in (0, 1, 3, 2):
            if count == 1:
                when((sector + 1 <= last) & jnp.logical_not(left_on))(lambda: arrived(tick, index, 1))
                when((sector + 3 <= last) & jnp.logical_not(right_on))(lambda: arrived(tick, index, 3))
            if count == 2:
                meanwhile()
                when(sector + 2 <= last)(lambda: arrived(tick, index, 2))
            block_high, block_low = halves(slots[tick, index, count])
            both = jnp.dot(
                jnp.concatenate([block_high, block_low], axis=0), high[count], preferred_element_type=jnp.float32
            )
            rest = jnp.dot(block_high, low[count], preferred_element_type=jnp.float32)
            amplitude = (both[:rows] + (both[rows:] + rest)) * factor
            selected = jnp.where(choice == float(count), amplitude, selected)
            squares = squares + amplitude * amplitude

        @when((site < last_site) | (tick == ticks - 1))
        def _():
            picked[tick, index] = selected

        @when(tick < ticks - 1)
        def _():
            start(next_sends(tick, index))

        def folded(value):
            return sum(value[:, tile * LANES : (tile + 1) * LANES] for tile in range(tiles))

        picked_fold[part, :] = folded(selected * selected)
        total_fold[part, :] = folded(squares)

    for index in range(CHUNKS):
        start(first_sends(index))

    @when(site == last_site)
    def _():
        for tick in range(ticks - 1):
            for index in range(CHUNKS):
                entering_copy(tick, index).start()

    for count in range(1, 4):

        @when(sector + count > last)
        def _():
            def clear(number, carry):
                slots[number // CHUNKS, number % CHUNKS, count] = jnp.zeros((rows, width), jnp.float32)
                return carry

            lax.fori_loop(0, ticks * CHUNKS, clear, 0)

    for count in range(4):
        raw_copies[count].wait()

        def cut(step, carry):
            part = pl.ds(pl.multiple_of(step * 64, 64), 64)
            high[count, part, :], low[count, part, :] = halves(raw[count, part, :])
            return carry

        lax.fori_loop(0, width // 64, cut, 0)

    @when(site == last_site)
    def _():
        for tick in range(ticks - 1):
            for index in range(CHUNKS):
                entering_copy(tick, index).wait()

    steps = ticks * CHUNKS
    pass_on(0, 0)

    for copy in small_copies:
        copy.wait()

    def choose(tick, carry):
        chosen[tick] = column_of(outcomes[tick].astype(jnp.float32))
        return carry

    lax.fori_loop(0, ticks, choose, 0)

    for number in range(1, AHEAD):
        pass_on(number // CHUNKS, number % CHUNKS)

    def step(number, carry):
        tick, index = number // CHUNKS, number % CHUNKS
        later = number + AHEAD

        @when(index == 0)
        def _():
            begin(tick)

        def meanwhile():
            @when(later < steps)
            def _():
                pass_on(later // CHUNKS, later % CHUNKS)

        work(tick, index, meanwhile)

        @when((index == CHUNKS // 2 - 1) & (tick > 0))
        def _():
            middle(tick)

        @when(index == CHUNKS - 1)
        def _():
            end(tick)

        return carry

    lax.fori_loop(0, steps, step, 0)

    @when(site >= 1)
    def _():
        wait_for(along_y.at[ticks, pl.ds(0, side - 1)], y_sem.at[ticks])
        now_scale, now_log = advance(ticks)
        carried[ticks + 1, 2:3, :] = now_log
        carried[ticks + 1, 3:4, :] = now_scale
        scale[...] = column_of(now_scale)

    @when(site == 0)
    def _():
        carried[ticks + 1, 2:3, :] = carried[ticks, 2:3, :]
        carried[ticks + 1, 3:4, :] = carried[ticks, 3:4, :]

    wait_for(along_x.at[ticks, pl.ds(0, side - 1)], x_sem.at[ticks])
    carried[ticks + 1, 0:2, :] = four(along_x, ticks)[0:2]
    for copy in y_sends(ticks + 1, site)[1:]:
        copy.start()
    along_y[ticks + 1, y] = carried[ticks + 1]

    for index in range(CHUNKS):
        finish(first_sends(index))

    def drain(number, carry):
        tick, index = number // CHUNKS, number % CHUNKS
        finish([(condition, copy) for condition, _, copy in relays(tick, index)])

        @when(tick < ticks - 1)
        def _():
            finish(next_sends(tick, index))

        return carry

    lax.fori_loop(0, steps, drain, 0)

    def drain_sums(tick, carry):
        @when(site < last_site)
        def _():
            wait_for(along_x.at[0], x_send_sem.at[tick])

        @when((age_at(tick) >= 1) & (site < last_site))
        def _():
            wait_for(along_y.at[0], y_send_sem.at[tick + 1])

        return carry

    lax.fori_loop(0, ticks - 1, drain_sums, 0)
    wait_for(along_x.at[0, pl.ds(0, side - 1)], x_send_sem.at[ticks - 1])

    @when(site >= 1)
    def _():
        wait_for(along_y.at[0, pl.ds(0, side - 1)], y_send_sem.at[ticks])

    wait_for(along_y.at[0, pl.ds(0, side - 1)], y_send_sem.at[ticks + 1])

    wait_for(along_y.at[ticks + 1, pl.ds(0, side - 1)], y_sem.at[ticks + 1])
    now_scale, now_log = advance(ticks + 1)
    logp_out[...] = now_log
    factor = scale[...] * column_of(now_scale)
    for index in range(CHUNKS):
        part = factor[index * rows : (index + 1) * rows]
        env_out[0, index * rows : (index + 1) * rows, :] = picked[ticks - 1, index] * jnp.concatenate([part] * tiles, axis=1)


def solution(mesh):
    sites, sectors = mesh.shape["site"], mesh.shape["sector"]
    side = int(round(sectors**0.5))

    def per_device(site_tensor, outcomes, in_flight, prior_logp, entering):
        ticks = outcomes.shape[0]
        _, counts, _, width, _ = site_tensor.shape
        rows = in_flight.shape[1] // CHUNKS
        vmem = pl.BlockSpec(memory_space=pltpu.VMEM)
        f32, dma = jnp.float32, pltpu.SemaphoreType.DMA
        return pl.pallas_call(
            functools.partial(kernel, ticks, side, sites, float(width * sectors)),
            name="chain",
            out_shape=(
                jax.ShapeDtypeStruct(in_flight.shape, f32),
                jax.ShapeDtypeStruct(prior_logp.shape, f32),
            ),
            in_specs=[pl.BlockSpec(memory_space=pltpu.HBM)] * 5,
            out_specs=(vmem, vmem),
            scratch_shapes=[
                pltpu.VMEM(outcomes.shape, jnp.int32),
                pltpu.VMEM(prior_logp.shape, f32),
                pltpu.VMEM((counts, width, width), f32),
                pltpu.VMEM((counts, width, width), jnp.bfloat16),
                pltpu.VMEM((counts, width, width), jnp.bfloat16),
                pltpu.VMEM((ticks, CHUNKS, counts + 1, rows, width), f32),
                pltpu.VMEM((ticks, CHUNKS, rows, width), f32),
                pltpu.VMEM((ticks, LANES, LANES), f32),
                pltpu.VMEM((LANES, LANES), f32),
                pltpu.VMEM((LANES, LANES), f32),
                pltpu.VMEM((LANES, LANES), f32),
                pltpu.VMEM((ticks + 2, 4, LANES), f32),
                pltpu.VMEM((ticks, 4, LANES), f32),
                pltpu.VMEM((ticks + 1, side, 4, LANES), f32),
                pltpu.VMEM((ticks + 2, side, 4, LANES), f32),
                dma((counts,)),
                dma((2 + ticks * CHUNKS,)),
                dma((ticks, CHUNKS, counts + 1)),
                dma((ticks + 1,)),
                dma((ticks + 2,)),
                dma((7, ticks, CHUNKS)),
                dma((ticks,)),
                dma((ticks + 2,)),
            ],
            compiler_params=pltpu.CompilerParams(
                collective_id=0, has_side_effects=True, vmem_limit_bytes=60 * 1024 * 1024
            ),
            cost_estimate=pl.CostEstimate(
                flops=6 * ticks * counts * rows * CHUNKS * width * width,
                bytes_accessed=4 * counts * width * width,
                transcendentals=0,
            ),
        )(site_tensor, outcomes, in_flight, prior_logp, entering)

    return jax.shard_map(
        per_device,
        mesh=mesh,
        in_specs=(
            P("site", None, "sector", None, None),
            P(None, "site", None),
            P("site", None, "sector"),
            P("site", None),
            P(None, None, "sector"),
        ),
        out_specs=(P("site", None, "sector"), P("site", None)),
        check_vma=False,
    )
```

time: 119 us -> 93.4 us (0.78)
  the two profiles are of different devices: /device:TPU:32 before, /device:TPU:2 now
where the time goes in v2:
time: 93.4 us; the launch traced here: 93 us
  Pallas kernels  89.5 us (96%)
  local copies, waits for them, and re-layouts  2.8 us (3%)
    pallas_call x1, Pallas kernels, per_device(): pl.pallas_call(functools.partial(kernel, ticks, side, sites, float(width...  89.5 us
    unnamed x2, local copies, waits for them, and re-layouts  2.8 us

profile of v2, /device:TPU:2, one launch (start us, length us, event | category | flops | bytes accessed | tf_op | source)
XLA Modules:
  0.0 93.0 jit_solution(9079935874567210811)
XLA Ops:
  0.6 89.5 %chain.1 = (f32[1,128,512]{2,1,0:T(8,128)}, f32[1,128]{1,0:T(1,128)}) custom-call(f32[1,4,1,512,512]{4,3,2,1,0:T(8,128)} %site_tensor.1, s32[6,1,128]{2,1,0:T(1,128)} %outcomes_in.1, f32[1,128,512]{2,1,0:T(8,128)} %in_flight.1, f32[1,128]{1,0:T(1,128)} %prior_in.1, f32[5,128,512]{2,1,0:T(8,128)} %entering.1), custom_call_target="tpu_custom_call" | custom-call | flops 4831838208 | bytes 4194304 | tf_op jit(solution)/shard_map/chain/pallas_call | solution.py:494
  90.2 1.7 %copy.9 = f32[1,128,512]{2,1,0:T(8,128)} copy(f32[1,128,512]{2,1,0:T(8,128)} %get-tuple-element.4) | data formatting | bytes 524288
  91.8 1.1 %copy.10 = f32[1,128]{1,0:T(1,128)} copy(f32[1,128]{1,0:T(1,128)} %get-tuple-element.5) | data formatting | bytes 1024

commit v3 on v2

--- a/solution.py
+++ b/solution.py
@@ -66,14 +66,17 @@
     message,
     along_x,
     along_y,
+    along_all,
     raw_sem,
     local_sem,
     slot_sem,
     x_sem,
     y_sem,
+    all_sem,
     send_sem,
     x_send_sem,
     y_send_sem,
+    all_send_sem,
 ):
     site, sector = lax.axis_index("site"), lax.axis_index("sector")
     x, y = sector % side, sector // side
@@ -116,14 +119,15 @@
 
         return to_condition.astype(jnp.int32)
 
-    for near, own in ((site, False), (site_before, True)):
-        for hop in range(0 if own else 1, side):
-            expected += greet(always, (near, y * side + (x + hop) % side), always)
-        for hop in range(1, side):
-            expected += greet(always, (near, (y + hop) % side * side + x), always)
-        expected += greet((x == side - 1) & (sector < last), (near, sector + 1), (x == 0) & (sector > 0))
-        expected += greet((x != 0) & (sector + 3 <= last), (near, sector + 3), (x != side - 1) & (sector >= 3))
-    expected += greet((x == 0) & (sector > 0), (site, sector - 1), (x == side - 1) & (sector < last))
+    for hop in range(side):
+        expected += greet(always, (site_before, y * side + (x + hop) % side), always)
+    for hop in range(1, side):
+        expected += greet(always, (site_before, (y + hop) % side * side + x), always)
+    expected += greet((x == side - 1) & (sector < last), (site_before, sector + 1), (x == 0) & (sector > 0))
+    expected += greet((x != 0) & (sector + 3 <= last), (site_before, sector + 3), (x != side - 1) & (sector >= 3))
+    expected += greet(sector == last, (site_before, 0 * sector + 2), sector == 2)
+    for hop in range(1, last + 1):
+        expected += greet(always, (site, (sector + hop) % (last + 1)), always)
 
     for copy in row_copies + small_copies + raw_copies:
         copy.start()
@@ -145,11 +149,15 @@
     def sends(source, tick, index, to_site, odd):
         first_column = odd & (x == 0)
         third_column = odd & (x == 2)
+        to_left = (sector >= 1) & jnp.logical_not(first_column)
+        left = remote(source, tick, index, 1, 0, (to_site, sector - 1))
+        left_first = odd == (x >= 2)
         return [
-            ((sector >= 1) & jnp.logical_not(first_column), remote(source, tick, index, 1, 0, (to_site, sector - 1))),
+            (to_left & left_first, left),
             ((sector >= 3) & jnp.logical_not(third_column), remote(source, tick, index, 3, 1, (to_site, sector - 3))),
             ((sector >= side) & (first_column | third_column), remote(source, tick, index, 4, 2, (to_site, sector - side))),
-            ((sector == 2) & jnp.logical_not(odd), remote(source, tick, index, 4, 2, (to_site, sector + 1))),
+            ((sector == 2) & jnp.logical_not(odd), remote(source, tick, index, 4, 2, (to_site, last))),
+            (to_left & jnp.logical_not(left_first), left),
         ]
 
     def first_sends(index):
@@ -167,14 +175,14 @@
     right_on = (sector + 3 <= last) & jnp.logical_not(by_left(sector + 3))
     crossed = jnp.logical_not(even) & (sector + side <= last)
     stage_first, stage_third = crossed & (x == 0), crossed & (x == 2)
-    stage_two = even & (sector == 3)
+    stage_two = even & (sector == last)
 
     def relays(tick, index):
         stage, one, three = slots.at[tick, index, 4], slots.at[tick, index, 1], slots.at[tick, index, 3]
         return [
             (stage_first, 4, remote(stage, tick, index, 1, 4, (site, sector + 3))),
             (stage_third, 4, remote(stage, tick, index, 3, 4, (site, sector + 1))),
-            (stage_two, 4, remote(stage, tick, index, 2, 4, (site, sector - 3))),
+            (stage_two, 4, remote(stage, tick, index, 2, 4, (site, 0 * sector))),
             (left_on, 1, remote(one, tick, index, 2, 5, (site, sector - 1))),
             (right_on, 3, remote(three, tick, index, 2, 6, (site, sector + 1))),
         ]
@@ -216,20 +224,34 @@
             for hop in range(side)
         ]
 
+    def all_sends():
+        return [
+            pltpu.make_async_remote_copy(
+                src_ref=message.at[ticks - 1],
+                dst_ref=along_all.at[sector],
+                send_sem=all_send_sem.at[0],
+                recv_sem=all_sem.at[0],
+                device_id=(site, (sector + hop) % (last + 1)),
+                device_id_type=MESH,
+            )
+            for hop in range(1, last + 1)
+        ]
+
     def wait_for(ref, sem):
         pltpu.make_async_copy(ref, ref, sem).wait()
 
     def four(ref, tick):
         return (ref[tick, 0] + ref[tick, 1]) + (ref[tick, 2] + ref[tick, 3])
 
-    def advance(slot):
-        sums = four(along_y, slot)
-        before = along_y[slot, 0]
-        before_log, before_scale = before[2:3], before[3:4]
+    def advance(sums, before_log, before_scale):
         picked_power = sums[0:1] * before_scale * before_scale / bond + EPSILON
         total_power = sums[1:2] * before_scale * before_scale / bond + EPSILON
         return 1.0 / jnp.sqrt(picked_power), before_log + jnp.log(picked_power) - jnp.log(total_power)
 
+    def advance_from(slot):
+        before = along_y[slot, 0]
+        return advance(four(along_y, slot), before[2:3], before[3:4])
+
     def age_at(tick):
         return jnp.minimum(tick, site)
 
@@ -239,7 +261,7 @@
         @when(age >= 2)
         def _():
             wait_for(along_y.at[tick], y_sem.at[tick])
-            now_scale, now_log = advance(tick)
+            now_scale, now_log = advance_from(tick)
             carried[tick + 1, 2:3, :] = now_log
             carried[tick + 1, 3:4, :] = now_scale
             scale[...] = column_of(now_scale)
@@ -285,9 +307,9 @@
 
         @when(tick == ticks - 1)
         def _():
-            for copy in x_sends(tick, site)[1:]:
+            for copy in all_sends():
                 copy.start()
-            along_x[ticks, x] = message[ticks - 1]
+            along_all[sector] = message[ticks - 1]
 
     def pass_on(tick, index):
         for condition, count, copy in relays(tick, index):
@@ -421,7 +443,7 @@
     @when(site >= 1)
     def _():
         wait_for(along_y.at[ticks, pl.ds(0, side - 1)], y_sem.at[ticks])
-        now_scale, now_log = advance(ticks)
+        now_scale, now_log = advance_from(ticks)
         carried[ticks + 1, 2:3, :] = now_log
         carried[ticks + 1, 3:4, :] = now_scale
         scale[...] = column_of(now_scale)
@@ -431,12 +453,6 @@
         carried[ticks + 1, 2:3, :] = carried[ticks, 2:3, :]
         carried[ticks + 1, 3:4, :] = carried[ticks, 3:4, :]
 
-    wait_for(along_x.at[ticks, pl.ds(0, side - 1)], x_sem.at[ticks])
-    carried[ticks + 1, 0:2, :] = four(along_x, ticks)[0:2]
-    for copy in y_sends(ticks + 1, site)[1:]:
-        copy.start()
-    along_y[ticks + 1, y] = carried[ticks + 1]
-
     for index in range(CHUNKS):
         finish(first_sends(index))
 
@@ -464,16 +480,18 @@
         return carry
 
     lax.fori_loop(0, ticks - 1, drain_sums, 0)
-    wait_for(along_x.at[0, pl.ds(0, side - 1)], x_send_sem.at[ticks - 1])
-
     @when(site >= 1)
     def _():
         wait_for(along_y.at[0, pl.ds(0, side - 1)], y_send_sem.at[ticks])
 
-    wait_for(along_y.at[0, pl.ds(0, side - 1)], y_send_sem.at[ticks + 1])
-
-    wait_for(along_y.at[ticks + 1, pl.ds(0, side - 1)], y_sem.at[ticks + 1])
-    now_scale, now_log = advance(ticks + 1)
+    all_but_one = along_all.at[pl.ds(0, last)]
+    wait_for(all_but_one, all_send_sem.at[0])
+    wait_for(all_but_one, all_sem.at[0])
+    last_sums = [along_all[of_sector] for of_sector in range(side * side)]
+    while len(last_sums) > 1:
+        last_sums = [one + other for one, other in zip(last_sums[::2], last_sums[1::2])]
+    last_sums = last_sums[0]
+    now_scale, now_log = advance(last_sums, carried[ticks + 1, 2:3, :], carried[ticks + 1, 3:4, :])
     logp_out[...] = now_log
     factor = scale[...] * column_of(now_scale)
     for index in range(CHUNKS):
@@ -514,26 +532,34 @@
                 pltpu.VMEM((LANES, LANES), f32),
                 pltpu.VMEM((ticks + 2, 4, LANES), f32),
                 pltpu.VMEM((ticks, 4, LANES), f32),
+                pltpu.VMEM((ticks, side, 4, LANES), f32),
                 pltpu.VMEM((ticks + 1, side, 4, LANES), f32),
-                pltpu.VMEM((ticks + 2, side, 4, LANES), f32),
+                pltpu.VMEM((side * side, 4, LANES), f32),
                 dma((counts,)),
                 dma((2 + ticks * CHUNKS,)),
                 dma((ticks, CHUNKS, counts + 1)),
+                dma((ticks,)),
                 dma((ticks + 1,)),
-                dma((ticks + 2,)),
+                dma((1,)),
                 dma((7, ticks, CHUNKS)),
                 dma((ticks,)),
-                dma((ticks + 2,)),
+                dma((ticks + 1,)),
+                dma((1,)),
             ],
             compiler_params=pltpu.CompilerParams(
-                collective_id=0, has_side_effects=True, vmem_limit_bytes=60 * 1024 * 1024
+                collective_id=0, has_side_effects=True, vmem_limit_bytes=48 * 1024 * 1024
             ),
             cost_estimate=pl.CostEstimate(
                 flops=6 * ticks * counts * rows * CHUNKS * width * width,
                 bytes_accessed=4 * counts * width * width,
                 transcendentals=0,
             ),
-        )(site_tensor, outcomes, in_flight, prior_logp, entering)
+        )(
+            *(
+                pltpu.with_memory_space_constraint(array, pltpu.HBM)
+                for array in (site_tensor, outcomes, in_flight, prior_logp, entering)
+            )
+        )
 
     return jax.shard_map(
         per_device,

time: 93.4 us -> 86.1 us (0.922)
  Pallas kernels: 89.5 us -> 84.1 us
  local copies, waits for them, and re-layouts: 2.8 us -> 1.22 us
    pallas_call x1, Pallas kernels: 89.5 us -> 84.1 us  [per_device(): pl.pallas_call(functools.partial(kernel, ticks, side, sites, float(width...]
    unnamed x2, local copies, waits for them, and re-layouts: 2.8 us -> 1.22 us
where the time goes in v3:
time: 86.1 us; the launch traced here: 85.9 us
  Pallas kernels  84.1 us (98%)
  local copies, waits for them, and re-layouts  1.22 us (1%)
    pallas_call x1, Pallas kernels, per_device(): pl.pallas_call(functools.partial(kernel, ticks, side, sites, float(width...  84.1 us

profile of v3, /device:TPU:2, one launch (start us, length us, event | category | flops | bytes accessed | tf_op | source)
XLA Modules:
  0.0 85.9 jit_solution(308076185175241551)
XLA Ops:
  0.6 84.1 %chain.1 = (f32[1,128,512]{2,1,0:T(8,128)S(1)}, f32[1,128]{1,0:T(1,128)S(1)}) custom-call(f32[1,4,1,512,512]{4,3,2,1,0:T(8,128)} %site_tensor.1, s32[6,1,128]{2,1,0:T(1,128)} %outcomes_in.1, f32[1,128,512]{2,1,0:T(8,128)} %in_flight.1, f32[1,128]{1,0:T(1,128)} %prior_in.1, f32[5,128,512]{2,1,0:T(8,128)} %entering.1), custom_call_target="tpu_custom_call" | custom-call | flops 4831838208 | bytes 4194304 | tf_op jit(solution)/shard_map/chain/pallas_call | solution.py:512
  84.7 0.7 copy.9
  85.4 0.5 copy.10

commit v4 on v3

--- a/solution.py
+++ b/solution.py
@@ -132,6 +132,16 @@
     for copy in row_copies + small_copies + raw_copies:
         copy.start()
 
+    for count in range(4):
+        raw_copies[count].wait()
+
+        def cut(step, carry):
+            part = pl.ds(pl.multiple_of(step * 64, 64), 64)
+            high[count, part, :], low[count, part, :] = halves(raw[count, part, :])
+            return carry
+
+        lax.fori_loop(0, width // 64, cut, 0)
+
     pl.semaphore_wait(barrier, expected)
 
     def remote(source, tick, index, count, kind, where):
@@ -257,6 +267,7 @@
 
     def begin(tick):
         age = age_at(tick)
+        chosen[...] = column_of(outcomes[tick].astype(jnp.float32))
 
         @when(age >= 2)
         def _():
@@ -270,7 +281,7 @@
         def _():
             carried[tick + 1, 2:3, :] = jnp.where(tick == 0, prior[...], 0.0)
             carried[tick + 1, 3:4, :] = jnp.ones((1, LANES), jnp.float32)
-            scale[...] = jnp.ones_like(scale)
+            scale[...] = jnp.ones((LANES, LANES), jnp.float32)
 
     def middle(tick):
         @when(age_at(tick) >= 1)
@@ -330,7 +341,7 @@
 
         part = pl.ds(pl.multiple_of(index * rows, rows), rows)
         factor = jnp.concatenate([scale[part, :]] * tiles, axis=1)
-        choice = jnp.concatenate([chosen[tick, part, :]] * tiles, axis=1)
+        choice = jnp.concatenate([chosen[part, :]] * tiles, axis=1)
         selected = jnp.zeros((rows, width), jnp.float32)
         squares = jnp.zeros((rows, width), jnp.float32)
         for count in (0, 1, 3, 2):
@@ -363,7 +374,7 @@
         picked_fold[part, :] = folded(selected * selected)
         total_fold[part, :] = folded(squares)
 
-    for index in range(CHUNKS):
+    for index in range(AHEAD):
         start(first_sends(index))
 
     @when(site == last_site)
@@ -382,16 +393,6 @@
 
             lax.fori_loop(0, ticks * CHUNKS, clear, 0)
 
-    for count in range(4):
-        raw_copies[count].wait()
-
-        def cut(step, carry):
-            part = pl.ds(pl.multiple_of(step * 64, 64), 64)
-            high[count, part, :], low[count, part, :] = halves(raw[count, part, :])
-            return carry
-
-        lax.fori_loop(0, width // 64, cut, 0)
-
     @when(site == last_site)
     def _():
         for tick in range(ticks - 1):
@@ -400,18 +401,16 @@
 
     steps = ticks * CHUNKS
     pass_on(0, 0)
+    start(first_sends(AHEAD))
 
     for copy in small_copies:
         copy.wait()
 
-    def choose(tick, carry):
-        chosen[tick] = column_of(outcomes[tick].astype(jnp.float32))
-        return carry
-
-    lax.fori_loop(0, ticks, choose, 0)
-
-    for number in range(1, AHEAD):
-        pass_on(number // CHUNKS, number % CHUNKS)
+    for number in range(1, CHUNKS - AHEAD):
+        pass_on(0, number)
+        start(first_sends(AHEAD + number))
+    for number in range(CHUNKS - AHEAD, AHEAD):
+        pass_on(0, number)
 
     def step(number, carry):
         tick, index = number // CHUNKS, number % CHUNKS
@@ -526,7 +525,7 @@
                 pltpu.VMEM((counts, width, width), jnp.bfloat16),
                 pltpu.VMEM((ticks, CHUNKS, counts + 1, rows, width), f32),
                 pltpu.VMEM((ticks, CHUNKS, rows, width), f32),
-                pltpu.VMEM((ticks, LANES, LANES), f32),
+                pltpu.VMEM((LANES, LANES), f32),
                 pltpu.VMEM((LANES, LANES), f32),
                 pltpu.VMEM((LANES, LANES), f32),
                 pltpu.VMEM((LANES, LANES), f32),

time: 86.1 us -> 84.8 us (0.985)
  Pallas kernels: 84.1 us -> 82.4 us
    pallas_call x1, Pallas kernels: 84.1 us -> 82.4 us  [per_device(): pl.pallas_call(functools.partial(kernel, ticks, side, sites, float(width...]
where the time goes in v4:
time: 84.8 us; the launch traced here: 84.2 us
  Pallas kernels  82.4 us (97%)
  local copies, waits for them, and re-layouts  1.22 us (1%)
    pallas_call x1, Pallas kernels, per_device(): pl.pallas_call(functools.partial(kernel, ticks, side, sites, float(width...  82.4 us

profile of v4, /device:TPU:2, one launch (start us, length us, event | category | flops | bytes accessed | tf_op | source)
XLA Modules:
  0.0 84.2 jit_solution(12070542140850388032)
XLA Ops:
  0.6 82.4 %chain.1 = (f32[1,128,512]{2,1,0:T(8,128)S(1)}, f32[1,128]{1,0:T(1,128)S(1)}) custom-call(f32[1,4,1,512,512]{4,3,2,1,0:T(8,128)} %site_tensor.1, s32[6,1,128]{2,1,0:T(1,128)} %outcomes_in.1, f32[1,128,512]{2,1,0:T(8,128)} %in_flight.1, f32[1,128]{1,0:T(1,128)} %prior_in.1, f32[5,128,512]{2,1,0:T(8,128)} %entering.1), custom_call_target="tpu_custom_call" | custom-call | flops 4831838208 | bytes 4194304 | tf_op jit(solution)/shard_map/chain/pallas_call | solution.py:511
  83.0 0.7 copy.9
  83.7 0.5 copy.10

commit v5 on v4

--- a/solution.py
+++ b/solution.py
@@ -412,6 +412,18 @@
     for number in range(CHUNKS - AHEAD, AHEAD):
         pass_on(0, number)
 
+    def drain(number, carry):
+        tick, index = number // CHUNKS, number % CHUNKS
+        finish([(condition, copy) for condition, _, copy in relays(tick, index)])
+
+        @when(tick < ticks - 1)
+        def _():
+            finish(next_sends(tick, index))
+
+        return carry
+
+    lag = 2 * CHUNKS
+
     def step(number, carry):
         tick, index = number // CHUNKS, number % CHUNKS
         later = number + AHEAD
@@ -426,6 +438,10 @@
                 pass_on(later // CHUNKS, later % CHUNKS)
 
         work(tick, index, meanwhile)
+
+        @when(number >= lag)
+        def _():
+            drain(number - lag, 0)
 
         @when((index == CHUNKS // 2 - 1) & (tick > 0))
         def _():
@@ -455,17 +471,7 @@
     for index in range(CHUNKS):
         finish(first_sends(index))
 
-    def drain(number, carry):
-        tick, index = number // CHUNKS, number % CHUNKS
-        finish([(condition, copy) for condition, _, copy in relays(tick, index)])
-
-        @when(tick < ticks - 1)
-        def _():
-            finish(next_sends(tick, index))
-
-        return carry
-
-    lax.fori_loop(0, steps, drain, 0)
+    lax.fori_loop(steps - lag, steps, drain, 0)
 
     def drain_sums(tick, carry):
         @when(site < last_site)

time: 84.8 us -> 85 us (level)
  no operation moved by 1% of the time
where the time goes in v5:
time: 85 us; the launch traced here: 84.9 us
  Pallas kernels  83 us (98%)
  local copies, waits for them, and re-layouts  1.22 us (1%)
    pallas_call x1, Pallas kernels, per_device(): pl.pallas_call(functools.partial(kernel, ticks, side, sites, float(width...  83 us

profile of v5, /device:TPU:2, one launch (start us, length us, event | category | flops | bytes accessed | tf_op | source)
XLA Modules:
  0.0 84.9 jit_solution(14718503158936627971)
XLA Ops:
  0.6 83.0 %chain.1 = (f32[1,128,512]{2,1,0:T(8,128)S(1)}, f32[1,128]{1,0:T(1,128)S(1)}) custom-call(f32[1,4,1,512,512]{4,3,2,1,0:T(8,128)} %site_tensor.1, s32[6,1,128]{2,1,0:T(1,128)} %outcomes_in.1, f32[1,128,512]{2,1,0:T(8,128)} %in_flight.1, f32[1,128]{1,0:T(1,128)} %prior_in.1, f32[5,128,512]{2,1,0:T(8,128)} %entering.1), custom_call_target="tpu_custom_call" | custom-call | flops 4831838208 | bytes 4194304 | tf_op jit(solution)/shard_map/chain/pallas_call | solution.py:517
  83.7 0.7 copy.9
  84.4 0.5 copy.10

commit v6 on v4

--- a/solution.py
+++ b/solution.py
@@ -340,10 +340,7 @@
             arrived(tick, index, 0)
 
         part = pl.ds(pl.multiple_of(index * rows, rows), rows)
-        factor = jnp.concatenate([scale[part, :]] * tiles, axis=1)
-        choice = jnp.concatenate([chosen[part, :]] * tiles, axis=1)
-        selected = jnp.zeros((rows, width), jnp.float32)
-        squares = jnp.zeros((rows, width), jnp.float32)
+        products = []
         for count in (0, 1, 3, 2):
             if count == 1:
                 when((sector + 1 <= last) & jnp.logical_not(left_on))(lambda: arrived(tick, index, 1))
@@ -356,7 +353,19 @@
                 jnp.concatenate([block_high, block_low], axis=0), high[count], preferred_element_type=jnp.float32
             )
             rest = jnp.dot(block_high, low[count], preferred_element_type=jnp.float32)
-            amplitude = (both[:rows] + (both[rows:] + rest)) * factor
+            product = both[:rows] + (both[rows:] + rest)
+            products.append((count, product))
+
+        @when(index == 0)
+        def _():
+            begin(tick)
+
+        factor = jnp.concatenate([scale[part, :]] * tiles, axis=1)
+        choice = jnp.concatenate([chosen[part, :]] * tiles, axis=1)
+        selected = jnp.zeros((rows, width), jnp.float32)
+        squares = jnp.zeros((rows, width), jnp.float32)
+        for count, product in products:
+            amplitude = product * factor
             selected = jnp.where(choice == float(count), amplitude, selected)
             squares = squares + amplitude * amplitude
 
@@ -415,10 +424,6 @@
     def step(number, carry):
         tick, index = number // CHUNKS, number % CHUNKS
         later = number + AHEAD
-
-        @when(index == 0)
-        def _():
-            begin(tick)
 
         def meanwhile():
             @when(later < steps)

time: 84.8 us -> 84.5 us (level)
  no operation moved by 1% of the time
where the time goes in v6:
time: 84.5 us; the launch traced here: 83.9 us
  Pallas kernels  82 us (97%)
  local copies, waits for them, and re-layouts  1.22 us (1%)
    pallas_call x1, Pallas kernels, per_device(): pl.pallas_call(functools.partial(kernel, ticks, side, sites, float(width...  82 us

profile of v6, /device:TPU:2, one launch (start us, length us, event | category | flops | bytes accessed | tf_op | source)
XLA Modules:
  0.0 83.9 jit_solution(8631716170431663825)
XLA Ops:
  0.6 82.0 %chain.1 = (f32[1,128,512]{2,1,0:T(8,128)S(1)}, f32[1,128]{1,0:T(1,128)S(1)}) custom-call(f32[1,4,1,512,512]{4,3,2,1,0:T(8,128)} %site_tensor.1, s32[6,1,128]{2,1,0:T(1,128)} %outcomes_in.1, f32[1,128,512]{2,1,0:T(8,128)} %in_flight.1, f32[1,128]{1,0:T(1,128)} %prior_in.1, f32[5,128,512]{2,1,0:T(8,128)} %entering.1), custom_call_target="tpu_custom_call" | custom-call | flops 4831838208 | bytes 4194304 | tf_op jit(solution)/shard_map/chain/pallas_call | solution.py:516
  82.7 0.7 copy.9
  83.4 0.5 copy.10
